TPU v7x, 512 devices: a whole 4x4x16 slice. The times are simulated.
512 devices in a mesh: blk: 256 (over y_lo, z, x, core), head: 2 (over y_hi).
Axes of the slice: x: 4, y: 4 (y_hi: 2, y_lo: 2; y = y_hi * 2 + y_lo), z: 16, core: 2. Of those that a mesh axis runs over, the one named last changes fastest.
Arguments:
- block_table: int32 [256, 2], P('blk'), may hold values from 0 to 511, as said below
- a_query: bfloat16 [6, 32, 98304], P(None, 'head', 'blk'), may hold values from -8 to 8
- b_query: bfloat16 [98304, 768], P(('blk', 'head')), may hold values from -60 to 60
- a_key: bfloat16 [2, 32, 98304], P(None, 'head', 'blk'), may hold values from -8 to 8
- b_key: bfloat16 [98304, 256], P(('blk', 'head')), may hold values from -6 to 6
- a_value: bfloat16 [2, 32, 98304], P(None, 'head', 'blk'), may hold values from -6 to 6
- b_value: bfloat16 [98304, 256], P(('blk', 'head')), may hold values from -6 to 6
Outputs:
- attended: bfloat16 [32, 98304, 128], P('head', 'blk')
- log_total: float32 [32, 98304], P('head', 'blk')
Inputs may be any that keep to these rules, and one draw needn't show every extreme that they name: `block_table`: row e holds a block b below 256 and the block 511 - b; every block of the sequence appears exactly once.
All inputs are finite; a program needn't handle non-finite values.
Results may differ from a plain program's by a relative error of at most 0.012.
The roundings to bfloat16 on the way count: a program that leaves them out, or rounds other values in their place, can miss the bound.
Values may be sent and summed in bfloat16 or wider, within the bound.
A program may use at most 64 MiB of HBM per device.

v0:
```python
import math

import jax
import jax.numpy as jnp
from jax import lax
from jax.sharding import PartitionSpec as P

STEPS = 4


masked_fill = -1e30


def from_behind(array, axis, by):
    peers = lax.axis_size(axis)
    return lax.ppermute(array, axis, [(i, (i + by) % peers) for i in range(peers)])


def build_heads(factor_a, factor_b, rank_size):
    row_total = factor_b.shape[0]
    blocked = factor_b.reshape(row_total, rank_size, -1)
    product = jnp.einsum("rht,trd->htd", factor_a, blocked, preferred_element_type=jnp.float32)
    return (product * (1.0 / rank_size)).astype(jnp.bfloat16)


def attend(carried, queries, key_heads, value_heads, visible, score_scale):
    head_count = queries.shape[0]
    group_size = math.gcd(head_count, 4)
    group_count = head_count // group_size

    def grouped(array):
        return array.reshape((group_count, group_size) + array.shape[1:])

    def one_group(pieces):
        running_max, running_sum, running_out, query_part, key_part, value_part = pieces
        scores = (
            jnp.einsum("hqd,hkd->hqk", query_part, key_part, preferred_element_type=jnp.float32)
            * score_scale
        )
        new_max = jnp.maximum(running_max, jnp.max(jnp.where(visible, scores, masked_fill), axis=2))
        weights = jnp.where(visible, jnp.exp(scores - new_max[..., None]), 0.0)
        rescale = jnp.exp(running_max - new_max)
        new_sum = running_sum * rescale + jnp.sum(weights, axis=2)
        added = jnp.einsum(
            "hqk,hkd->hqd",
            weights.astype(jnp.bfloat16),
            value_part,
            preferred_element_type=jnp.float32,
        )
        return (new_max, new_sum, running_out * rescale[..., None] + added)

    inputs = tuple(
        (
            grouped(array)
            for array in (carried[0], carried[1], carried[2], queries, key_heads, value_heads)
        )
    )
    results = lax.map(one_group, inputs)
    return tuple((array.reshape((head_count,) + array.shape[2:]) for array in results))


def on_device(block_table, a_query, b_query, a_key, b_key, a_value, b_value):
    query_rows, key_rows, value_rows = (
        lax.all_gather(b_query, "head", axis=0, tiled=True),
        lax.all_gather(b_key, "head", axis=0, tiled=True),
        lax.all_gather(b_value, "head", axis=0, tiled=True),
    )
    row_count = key_rows.shape[0]
    half_len = row_count // 2
    head_count = a_query.shape[1]
    rank_query = a_query.shape[0]
    rank_key = a_key.shape[0]
    head_size = key_rows.shape[1] // rank_key
    score_scale = 1.0 / math.sqrt(head_size)
    offsets = jnp.arange(half_len, dtype=jnp.int32)

    def positions(block_pair):
        return (block_pair[:, None] * half_len + offsets[None, :]).reshape(row_count)

    queries = build_heads(a_query, query_rows, rank_query)
    own_pair = block_table[0]
    query_places = positions(own_pair)
    own_keys = build_heads(a_key, key_rows, rank_key)
    own_values = build_heads(a_value, value_rows, rank_key)
    payload = (own_keys, own_values, block_table)

    def consume(carried, key_heads, value_heads, source_pair):
        key_places = positions(source_pair)
        visible = key_places[None, :] <= query_places[:, None]
        return attend(carried, queries, key_heads, value_heads, visible, score_scale)

    carried = (
        jnp.full((head_count, row_count), masked_fill, jnp.float32),
        jnp.zeros((head_count, row_count), jnp.float32),
        jnp.zeros((head_count, row_count, head_size), jnp.float32),
    )
    carried = consume(carried, own_keys, own_values, own_pair)
    moving = payload
    for offset in range(1, STEPS):
        moving = from_behind((moving[0], moving[1], moving[2]), "blk", 1)
        key_heads = moving[0]
        value_heads = moving[1]
        carried = consume(carried, key_heads, value_heads, moving[-1][0])
    running_max, running_sum, running_out = carried
    attended = (running_out / running_sum[..., None]).astype(jnp.bfloat16)
    log_total = running_max + jnp.log(running_sum)
    return (attended, log_total)


def solution(mesh):
    in_specs = (
        P("blk", None),
        P(None, "head", "blk"),
        P(("blk", "head"), None),
        P(None, "head", "blk"),
        P(("blk", "head"), None),
        P(None, "head", "blk"),
        P(("blk", "head"), None),
    )
    out_specs = (P("head", "blk", None), P("head", "blk"))
    return jax.shard_map(
        on_device, mesh=mesh, in_specs=in_specs, out_specs=out_specs, check_vma=False
    )
```

profile of v0, /device:TPU:24, one launch (start us, length us, event | category | flops | bytes accessed | tf_op | source)
XLA Modules:
  0.0 209.8 jit_solution(214361106015340552)
XLA Ops:
  0.7 7.1 %all_gather.11 = bf16[384,256]{1,0:T(8,128)(2,1)S(1)} all-gather(bf16[192,256]{1,0:T(8,128)(2,1)} %param.21), channel_id=1, replica_groups=mesh['blk'=256,'head'=2] {'head'}, dimensions={0}, use_global_device_ids=true | all-gather | bytes 294912 | tf_op jit(solution)/shard_map/all_gather | solution.py:66
  8.8 1.9 multiply_convert_fusion
  10.7 1.9 collective-permute-start.2
  12.6 7.3 %all_gather.10 = bf16[384,256]{1,0:T(8,128)(2,1)S(1)} all-gather(bf16[192,256]{1,0:T(8,128)(2,1)S(1)} %copy-done.2), channel_id=1, replica_groups=mesh['blk'=256,'head'=2] {'head'}, dimensions={0}, use_global_device_ids=true | all-gather | bytes 294912 | tf_op jit(solution)/shard_map/all_gather | solution.py:65
  20.1 1.9 multiply_convert_fusion.1
  22.0 2.3 %collective-permute-start.1 = (bf16[16,384,128]{2,0,1:T(8,128)(2,1)}, bf16[16,384,128]{2,0,1:T(8,128)(2,1)}, u32[]{:S(2)}, u32[]{:S(2)}) collective-permute-start(bf16[16,384,128]{2,0,1:T(8,128)(2,1)} %bitcast.3), channel_id=1, source_target_pairs={{0,2},{2,4},{4,6},{6,8},{8,10},{10,12},{12,14},{14,16},{16,18},{18... | collective-permute-start | bytes 4718600 | tf_op jit(solution)/shard_map/ppermute | solution.py:16
  24.3 3.1 %collective-permute-start = (s32[1,2]{1,0:T(1,128)S(1)}, s32[1,2]{1,0:T(1,128)S(1)}, u32[]{:S(2)}, u32[]{:S(2)}) collective-permute-start(s32[1,2]{1,0:T(1,128)S(1)} %copy-done.5), channel_id=1, source_target_pairs={{0,2},{2,4},{4,6},{6,8},{8,10},{10,12},{12,14},{14,16},{16,18},{18... | collective-permute-start | bytes 32 | tf_op jit(solution)/shard_map/ppermute | solution.py:16
  27.4 37.6 %all_gather.9 = bf16[384,768]{1,0:T(8,128)(2,1)S(1)} all-gather(bf16[192,768]{1,0:T(8,128)(2,1)S(1)} %copy-done.1), channel_id=1, replica_groups=mesh['blk'=256,'head'=2] {'head'}, dimensions={0}, use_global_device_ids=true | all-gather | bytes 884736 | tf_op jit(solution)/shard_map/all_gather | solution.py:64
  67.1 1.6 copy.58
  69.2 18.8 %while.60 = (s32[]{:T(128)}, f32[4,4,384]{2,1,0:T(4,128)S(1)}, f32[4,4,384]{2,1,0:T(4,128)S(1)}, f32[4,4,384,128]{3,2,1,0:T(8,128)S(1)}, bf16[4,4,384,128]{3,2,1...) while((s32[]{:T(128)}, f32[4,4,384]{2,1,0:T(4,128)S(1)}, ...), condition=%wide.region_3.4_spmd.clone, body=%wide.region_0.3_spmd.clone.sunk | while | flops 308829696 | bytes 11282537 | solution.py:58
  69.2 1.4 constant_dynamic-slice_fusion.12
  70.7 1.6 select_reduce_fusion.8
  73.9 1.4 constant_dynamic-slice_fusion.12
  75.4 1.6 select_reduce_fusion.8
  78.6 1.4 constant_dynamic-slice_fusion.12
  80.1 1.6 select_reduce_fusion.8
  83.3 1.4 constant_dynamic-slice_fusion.12
  84.8 1.6 select_reduce_fusion.8
  88.1 2.0 collective-permute-start.3
  90.1 7.1 %collective-permute-done.3 = s32[1,2]{1,0:T(1,128)S(1)} collective-permute-done((s32[1,2]{1,0:T(1,128)S(1)}, s32[1,2]{1,0:T(1,128)S(1)}, u32[]{:S(2)}, u32[]{:S(2)}) %collective-permute-start.3) | collective-permute-done | bytes 40 | tf_op jit(solution)/shard_map/ppermute | solution.py:16
  97.4 1.9 collective-permute-start.6
  99.3 7.2 %collective-permute-done.6 = s32[1,2]{1,0:T(1,128)S(1)} collective-permute-done((s32[1,2]{1,0:T(1,128)S(1)}, s32[1,2]{1,0:T(1,128)S(1)}, u32[]{:S(2)}, u32[]{:S(2)}) %collective-permute-start.6) | collective-permute-done | bytes 40 | tf_op jit(solution)/shard_map/ppermute | solution.py:16
  106.6 1.9 collective-permute-start.4
  108.5 1.9 collective-permute-start.5
  110.4 2.0 broadcast.126.clone.1
  112.4 22.3 %while.61 = (s32[]{:T(128)}, f32[4,4,384]{2,1,0:T(4,128)S(1)}, f32[4,4,384]{2,1,0:T(4,128)S(1)}, f32[4,4,384,128]{3,2,1,0:T(8,128)}, f32[4,4,384]{2,1,0:T(4,128)...) while((s32[]{:T(128)}, f32[4,4,384]{2,1,0:T(4,128)S(1)}, ...), condition=%wide.region_7.8_spmd.clone, body=%wide.region_4.7_spmd.clone.sunk | while | flops 309024768 | bytes 12089481 | solution.py:58
  112.4 1.4 constant_dynamic-slice_fusion.13
  114.0 1.6 select_reduce_fusion.9
  115.6 1.9 fusion.114
  118.0 1.4 constant_dynamic-slice_fusion.13
  119.6 1.6 select_reduce_fusion.9
  121.2 1.9 fusion.114
  123.6 1.4 constant_dynamic-slice_fusion.13
  125.2 1.6 select_reduce_fusion.9
  126.8 1.8 fusion.114
  129.2 1.4 constant_dynamic-slice_fusion.13
  130.7 1.6 select_reduce_fusion.9
  132.3 1.9 fusion.114
  134.7 1.9 collective-permute-start.7
  136.7 13.0 %collective-permute-done.5 = bf16[16,384,128]{2,0,1:T(8,128)(2,1)} collective-permute-done((bf16[16,384,128]{2,0,1:T(8,128)(2,1)}, bf16[16,384,128]{2,0,1:T(8,128)(2,1)}, u32[]{:S(2)}, u32[]{:S(2)}) %collective-permute-start.5) | collective-permute-done | bytes 1572896 | tf_op jit(solution)/shard_map/ppermute | solution.py:16
  149.7 2.1 collective-permute-start.8
  152.1 23.3 %while.62 = (s32[]{:T(128)}, f32[4,4,384]{2,1,0:T(4,128)S(1)}, f32[4,4,384]{2,1,0:T(4,128)S(1)}, f32[4,4,384,128]{3,2,1,0:T(8,128)S(1)}, f32[4,4,384]{2,1,0:T(4,...) while((s32[]{:T(128)}, f32[4,4,384]{2,1,0:T(4,128)S(1)}, ...), condition=%wide.region_11.12_spmd.clone, body=%wide.region_8.11_spmd.clone.sunk | while | flops 309024768 | bytes 12088973 | solution.py:58
  152.1 1.4 constant_dynamic-slice_fusion.14
  153.7 1.6 select_reduce_fusion.10
  155.3 2.1 %fusion.119 = f32[4,4,384,128]{3,2,1,0:T(8,128)S(1)} fusion(f32[4,4,384,128]{3,2,1,0:T(8,128)S(1)} %get-tuple-element.1004, s32[]{:T(128)} %get-tuple-element.1001, f32[4,384,384]{1,2,0:T(8,128)S(1)} %get-tuple-element.895, f32[4,384]{1,0:T(4,128)S(1)} %get-tuple-element.897, pred[384,384]{0,1:T(8,128)(4,1)S(1)} %broadcast_compare_fusion.10, ...), kind=kOutput, calls=%fused_computation.70.clone.1 | convolution fusion | flops 153747456 | bytes 4485124 | tf_op jit(solution)/shard_map/while/body/eval_jaxpr/hqk,hkd->hqd/dot_general | solution.py:44
  158.0 1.4 constant_dynamic-slice_fusion.14
  159.5 1.6 select_reduce_fusion.10
  161.1 2.1 %fusion.119 = f32[4,4,384,128]{3,2,1,0:T(8,128)S(1)} fusion(f32[4,4,384,128]{3,2,1,0:T(8,128)S(1)} %get-tuple-element.1004, s32[]{:T(128)} %get-tuple-element.1001, f32[4,384,384]{1,2,0:T(8,128)S(1)} %get-tuple-element.895, f32[4,384]{1,0:T(4,128)S(1)} %get-tuple-element.897, pred[384,384]{0,1:T(8,128)(4,1)S(1)} %broadcast_compare_fusion.10, ...), kind=kOutput, calls=%fused_computation.70.clone.1 | convolution fusion | flops 153747456 | bytes 4485124 | tf_op jit(solution)/shard_map/while/body/eval_jaxpr/hqk,hkd->hqd/dot_general | solution.py:44
  163.8 1.4 constant_dynamic-slice_fusion.14
  165.4 1.6 select_reduce_fusion.10
  167.0 2.1 %fusion.119 = f32[4,4,384,128]{3,2,1,0:T(8,128)S(1)} fusion(f32[4,4,384,128]{3,2,1,0:T(8,128)S(1)} %get-tuple-element.1004, s32[]{:T(128)} %get-tuple-element.1001, f32[4,384,384]{1,2,0:T(8,128)S(1)} %get-tuple-element.895, f32[4,384]{1,0:T(4,128)S(1)} %get-tuple-element.897, pred[384,384]{0,1:T(8,128)(4,1)S(1)} %broadcast_compare_fusion.10, ...), kind=kOutput, calls=%fused_computation.70.clone.1 | convolution fusion | flops 153747456 | bytes 4485124 | tf_op jit(solution)/shard_map/while/body/eval_jaxpr/hqk,hkd->hqd/dot_general | solution.py:44
  171.2 1.6 select_reduce_fusion.10
  172.8 2.1 %fusion.119 = f32[4,4,384,128]{3,2,1,0:T(8,128)S(1)} fusion(f32[4,4,384,128]{3,2,1,0:T(8,128)S(1)} %get-tuple-element.1004, s32[]{:T(128)} %get-tuple-element.1001, f32[4,384,384]{1,2,0:T(8,128)S(1)} %get-tuple-element.895, f32[4,384]{1,0:T(4,128)S(1)} %get-tuple-element.897, pred[384,384]{0,1:T(8,128)(4,1)S(1)} %broadcast_compare_fusion.10, ...), kind=kOutput, calls=%fused_computation.70.clone.1 | convolution fusion | flops 153747456 | bytes 4485124 | tf_op jit(solution)/shard_map/while/body/eval_jaxpr/hqk,hkd->hqd/dot_general | solution.py:44
  175.5 7.9 %collective-permute-done.8 = bf16[16,384,128]{2,0,1:T(8,128)(2,1)} collective-permute-done((bf16[16,384,128]{2,0,1:T(8,128)(2,1)}, bf16[16,384,128]{2,0,1:T(8,128)(2,1)}, u32[]{:S(2)}, u32[]{:S(2)}) %collective-permute-start.8) | collective-permute-done | bytes 1572896 | tf_op jit(solution)/shard_map/ppermute | solution.py:16
  183.7 23.3 %while.63 = (s32[]{:T(128)}, f32[4,4,384]{2,1,0:T(4,128)S(1)}, f32[4,4,384]{2,1,0:T(4,128)S(1)}, f32[4,4,384,128]{3,2,1,0:T(8,128)S(1)}, f32[4,4,384]{2,1,0:T(4,...) while((s32[]{:T(128)}, f32[4,4,384]{2,1,0:T(4,128)S(1)}, ...), condition=%wide.region_15.16_spmd.clone, body=%wide.region_12.15_spmd.clone.sunk | while | flops 309024768 | bytes 12088973 | solution.py:58
  185.3 1.6 select_reduce_fusion.11
  186.9 2.1 %fusion.124 = f32[4,4,384,128]{3,2,1,0:T(8,128)S(1)} fusion(f32[4,4,384,128]{3,2,1,0:T(8,128)S(1)} %get-tuple-element.1043, s32[]{:T(128)} %get-tuple-element.1040, f32[4,384,384]{1,2,0:T(8,128)S(1)} %get-tuple-element.915, f32[4,384]{1,0:T(4,128)S(1)} %get-tuple-element.917, pred[384,384]{0,1:T(8,128)(4,1)S(1)} %broadcast_compare_fusion.11, ...), kind=kOutput, calls=%fused_computation.100.clone.1 | convolution fusion | flops 153747456 | bytes 4485124 | tf_op jit(solution)/shard_map/while/body/eval_jaxpr/hqk,hkd->hqd/dot_general | solution.py:44
  191.1 1.6 select_reduce_fusion.11
  192.7 2.1 %fusion.124 = f32[4,4,384,128]{3,2,1,0:T(8,128)S(1)} fusion(f32[4,4,384,128]{3,2,1,0:T(8,128)S(1)} %get-tuple-element.1043, s32[]{:T(128)} %get-tuple-element.1040, f32[4,384,384]{1,2,0:T(8,128)S(1)} %get-tuple-element.915, f32[4,384]{1,0:T(4,128)S(1)} %get-tuple-element.917, pred[384,384]{0,1:T(8,128)(4,1)S(1)} %broadcast_compare_fusion.11, ...), kind=kOutput, calls=%fused_computation.100.clone.1 | convolution fusion | flops 153747456 | bytes 4485124 | tf_op jit(solution)/shard_map/while/body/eval_jaxpr/hqk,hkd->hqd/dot_general | solution.py:44
  197.0 1.6 select_reduce_fusion.11
  198.6 2.1 %fusion.124 = f32[4,4,384,128]{3,2,1,0:T(8,128)S(1)} fusion(f32[4,4,384,128]{3,2,1,0:T(8,128)S(1)} %get-tuple-element.1043, s32[]{:T(128)} %get-tuple-element.1040, f32[4,384,384]{1,2,0:T(8,128)S(1)} %get-tuple-element.915, f32[4,384]{1,0:T(4,128)S(1)} %get-tuple-element.917, pred[384,384]{0,1:T(8,128)(4,1)S(1)} %broadcast_compare_fusion.11, ...), kind=kOutput, calls=%fused_computation.100.clone.1 | convolution fusion | flops 153747456 | bytes 4485124 | tf_op jit(solution)/shard_map/while/body/eval_jaxpr/hqk,hkd->hqd/dot_general | solution.py:44
  202.8 1.6 select_reduce_fusion.11
  204.4 2.1 %fusion.124 = f32[4,4,384,128]{3,2,1,0:T(8,128)S(1)} fusion(f32[4,4,384,128]{3,2,1,0:T(8,128)S(1)} %get-tuple-element.1043, s32[]{:T(128)} %get-tuple-element.1040, f32[4,384,384]{1,2,0:T(8,128)S(1)} %get-tuple-element.915, f32[4,384]{1,0:T(4,128)S(1)} %get-tuple-element.917, pred[384,384]{0,1:T(8,128)(4,1)S(1)} %broadcast_compare_fusion.11, ...), kind=kOutput, calls=%fused_computation.100.clone.1 | convolution fusion | flops 153747456 | bytes 4485124 | tf_op jit(solution)/shard_map/while/body/eval_jaxpr/hqk,hkd->hqd/dot_general | solution.py:44
  207.7 2.1 fusion.80
  (124 shorter events, 27.6 us)
Async XLA Ops:
  0.6 11.9 %copy-start.2 = (bf16[192,256]{1,0:T(8,128)(2,1)S(1)}, bf16[192,256]{1,0:T(8,128)(2,1)}, u32[]{:S(2)}) copy-start(bf16[192,256]{1,0:T(8,128)(2,1)} %param.19) | copy-start | bytes 294916
  0.6 19.3 %copy-start.4 = (bf16[2,16,384]{2,1,0:T(8,128)(2,1)S(1)}, bf16[2,16,384]{2,1,0:T(8,128)(2,1)}, u32[]{:S(2)}) copy-start(bf16[2,16,384]{2,1,0:T(8,128)(2,1)} %param.18) | copy-start | bytes 73732
  8.8 15.5 %copy-start.5 = (s32[1,2]{1,0:T(1,128)S(1)}, s32[1,2]{1,0:T(1,128)}, u32[]{:S(2)}) copy-start(s32[1,2]{1,0:T(1,128)} %param.15) | copy-start | bytes 28
  8.8 18.7 %copy-start.1 = (bf16[192,768]{1,0:T(8,128)(2,1)S(1)}, bf16[192,768]{1,0:T(8,128)(2,1)}, u32[]{:S(2)}) copy-start(bf16[192,768]{1,0:T(8,128)(2,1)} %param.17) | copy-start | bytes 884740
  10.7 97.8 %collective-permute-start.2 = (bf16[16,384,128]{2,0,1:T(8,128)(2,1)}, bf16[16,384,128]{2,0,1:T(8,128)(2,1)}, u32[]{:S(2)}, u32[]{:S(2)}) collective-permute-start(bf16[16,384,128]{2,0,1:T(8,128)(2,1)} %bitcast.5), channel_id=1, source_target_pairs={{0,2},{2,4},{4,6},{6,8},{8,10},{10,12},{12,14},{14,16},{16,18},{18... | collective-permute-start | bytes 4718600 | tf_op jit(solution)/shard_map/ppermute | solution.py:16
  20.1 45.7 %copy-start.3 = (bf16[6,16,384]{2,1,0:T(8,128)(2,1)S(1)}, bf16[6,16,384]{2,1,0:T(8,128)(2,1)}, u32[]{:S(2)}) copy-start(bf16[6,16,384]{2,1,0:T(8,128)(2,1)} %param.16) | copy-start | bytes 221188
  22.0 84.6 %collective-permute-start.1 = (bf16[16,384,128]{2,0,1:T(8,128)(2,1)}, bf16[16,384,128]{2,0,1:T(8,128)(2,1)}, u32[]{:S(2)}, u32[]{:S(2)}) collective-permute-start(bf16[16,384,128]{2,0,1:T(8,128)(2,1)} %bitcast.3), channel_id=1, source_target_pairs={{0,2},{2,4},{4,6},{6,8},{8,10},{10,12},{12,14},{14,16},{16,18},{18... | collective-permute-start | bytes 4718600 | tf_op jit(solution)/shard_map/ppermute | solution.py:16
  24.3 63.7 %collective-permute-start = (s32[1,2]{1,0:T(1,128)S(1)}, s32[1,2]{1,0:T(1,128)S(1)}, u32[]{:S(2)}, u32[]{:S(2)}) collective-permute-start(s32[1,2]{1,0:T(1,128)S(1)} %copy-done.5), channel_id=1, source_target_pairs={{0,2},{2,4},{4,6},{6,8},{8,10},{10,12},{12,14},{14,16},{16,18},{18... | collective-permute-start | bytes 32 | tf_op jit(solution)/shard_map/ppermute | solution.py:16
  88.1 9.1 %collective-permute-start.3 = (s32[1,2]{1,0:T(1,128)S(1)}, s32[1,2]{1,0:T(1,128)S(1)}, u32[]{:S(2)}, u32[]{:S(2)}) collective-permute-start(s32[1,2]{1,0:T(1,128)S(1)} %collective-permute-done), channel_id=1, source_target_pairs={{0,2},{2,4},{4,6},{6,8},{8,10},{10,12},{12,14},{14,16},{16,18},{18... | collective-permute-start | bytes 32 | tf_op jit(solution)/shard_map/ppermute | solution.py:16
  97.4 9.1 %collective-permute-start.6 = (s32[1,2]{1,0:T(1,128)S(1)}, s32[1,2]{1,0:T(1,128)S(1)}, u32[]{:S(2)}, u32[]{:S(2)}) collective-permute-start(s32[1,2]{1,0:T(1,128)S(1)} %collective-permute-done.3), channel_id=1, source_target_pairs={{0,2},{2,4},{4,6},{6,8},{8,10},{10,12},{12,14},{14,16},{16,18},{18... | collective-permute-start | bytes 32 | tf_op jit(solution)/shard_map/ppermute | solution.py:16
  106.6 28.1 %collective-permute-start.4 = (bf16[16,384,128]{2,0,1:T(8,128)(2,1)}, bf16[16,384,128]{2,0,1:T(8,128)(2,1)}, u32[]{:S(2)}, u32[]{:S(2)}) collective-permute-start(bf16[16,384,128]{2,0,1:T(8,128)(2,1)} %collective-permute-done.1), channel_id=1, source_target_pairs={{0,2},{2,4},{4,6},{6,8},{8,10},{10,12},{12,14},{14,16},{16,18},{18... | collective-permute-start | bytes 4718600 | tf_op jit(solution)/shard_map/ppermute | solution.py:16
  108.5 41.2 %collective-permute-start.5 = (bf16[16,384,128]{2,0,1:T(8,128)(2,1)}, bf16[16,384,128]{2,0,1:T(8,128)(2,1)}, u32[]{:S(2)}, u32[]{:S(2)}) collective-permute-start(bf16[16,384,128]{2,0,1:T(8,128)(2,1)} %collective-permute-done.2), channel_id=1, source_target_pairs={{0,2},{2,4},{4,6},{6,8},{8,10},{10,12},{12,14},{14,16},{16,18},{18... | collective-permute-start | bytes 4718600 | tf_op jit(solution)/shard_map/ppermute | solution.py:16
  134.7 40.8 %collective-permute-start.7 = (bf16[16,384,128]{2,0,1:T(8,128)(2,1)}, bf16[16,384,128]{2,0,1:T(8,128)(2,1)}, u32[]{:S(2)}, u32[]{:S(2)}) collective-permute-start(bf16[16,384,128]{2,0,1:T(8,128)(2,1)} %collective-permute-done.4), channel_id=1, source_target_pairs={{0,2},{2,4},{4,6},{6,8},{8,10},{10,12},{12,14},{14,16},{16,18},{18... | collective-permute-start | bytes 4718600 | tf_op jit(solution)/shard_map/ppermute | solution.py:16
  149.7 33.7 %collective-permute-start.8 = (bf16[16,384,128]{2,0,1:T(8,128)(2,1)}, bf16[16,384,128]{2,0,1:T(8,128)(2,1)}, u32[]{:S(2)}, u32[]{:S(2)}) collective-permute-start(bf16[16,384,128]{2,0,1:T(8,128)(2,1)} %collective-permute-done.5), channel_id=1, source_target_pairs={{0,2},{2,4},{4,6},{6,8},{8,10},{10,12},{12,14},{14,16},{16,18},{18... | collective-permute-start | bytes 4718600 | tf_op jit(solution)/shard_map/ppermute | solution.py:16
  175.5 7.9 %copy-start = (f32[4,4,384,128]{3,2,1,0:T(8,128)}, f32[4,4,384,128]{3,2,1,0:T(8,128)S(1)}, u32[]{:S(2)}) copy-start(f32[4,4,384,128]{3,2,1,0:T(8,128)S(1)} %get-tuple-element.1035) | copy-start | bytes 9437188
where the time goes:
time: 212 us; the launch traced here: 210 us
  matrix products  58.1 us (27%)
  blocking collectives  52 us (25%)
  waiting for transfers between devices  35.2 us (17%)
  local copies, waits for them, and re-layouts  29.5 us (14%)
  starting transfers between devices  19 us (9%)
  other arithmetic  14.2 us (7%)
    all_gather x1, blocking collectives, on_device(): lax.all_gather(b_query, 'head', axis=0, tiled=True)  37.6 us
    ppermute x9, waiting for transfers between devices, from_behind(): lax.ppermute(array, axis, [(i, (i + by) % peers) for i in range(peers)])  35.2 us
    dot_general x16, matrix products, one_group(): jnp.einsum('hqk,hkd->hqd', weights.astype(jnp.bfloat16), value_part, pref...  28.3 us
    dot_general x16, matrix products, one_group(): jnp.einsum('hqd,hkd->hqk', query_part, key_part, preferred_element_type=j...  25.3 us
    dynamic_slice x16, local copies, waits for them, and re-layouts, attend(): results = lax.map(one_group, inputs)  22.2 us
    ppermute x9, starting transfers between devices, from_behind(): lax.ppermute(array, axis, [(i, (i + by) % peers) for i in range(peers)])  19 us
    reduce_sum x16, other arithmetic, one_group(): new_sum = running_sum * rescale + jnp.sum(weights, axis=2)  8.24 us
    all_gather x1, blocking collectives, on_device(): lax.all_gather(b_key, 'head', axis=0, tiled=True)  7.28 us
  transfers between devices with their start and end apart: 9, of which 4 were waited for; matrix products, arithmetic and copies ran while one was open for 35% of the time, Pallas kernels for 0%

commit v1 on v0

v1 whole, which is shorter than its diff:
```python
import math

import jax
import jax.numpy as jnp
from jax import lax
from jax.experimental import pallas as pl
from jax.experimental.pallas import tpu as pltpu
from jax.sharding import PartitionSpec as P

HALF = 192
DH = 128
PAIRS = 8
RQ = 6
MESH = pl.DeviceIdType.MESH
F32 = jnp.float32
BF16 = jnp.bfloat16
SCALE = 0.5 / math.sqrt(DH)
SCALE2 = SCALE * math.log2(math.e)
MASKED = -1e30


def kernel(
    bt_in, aq_in, bq_in, ak_in, bk_in, av_in, bv_in,
    out_ref, log_ref,
    bt, bts, aq, bq, bkv, akv,
    bqt, a2q, qbd, bkf, bvt, akt, avj,
    o_own, m_own, l_own, o_acc, m_acc, l_acc, logs,
    local_sem, bts_sem, ex_send, ex_recv, a_send, a_recv, f_send, f_recv, t_send, t_recv, b_send, b_recv,
):
    e = lax.axis_index("blk")
    h = lax.axis_index("head")
    places = lax.axis_size("blk")
    other = 1 - h
    core = lax.rem(e, 2)
    lane = lax.broadcasted_iota(jnp.int32, (1, 2 * HALF), 1)
    first = lane < HALF

    def at(blk, head):
        return {"blk": lax.rem(blk + places, places), "head": head}

    barrier = pltpu.get_barrier_semaphore()
    pl.semaphore_signal(barrier, inc=1, device_id=at(e - 1, h), device_id_type=MESH)
    pl.semaphore_signal(barrier, inc=1, device_id=at(e, other), device_id_type=MESH)

    @pl.when(core == 0)
    def _():
        pl.semaphore_signal(barrier, inc=1, device_id=at(e - 2, h), device_id_type=MESH)

    locals_ = [
        pltpu.make_async_copy(src, dst, local_sem.at[i])
        for i, (src, dst) in enumerate(
            [
                (bk_in, bkv.at[0, h, 0]),
                (bv_in, bkv.at[0, h, 1]),
                (ak_in, akv.at[0, pl.ds(0, 2)]),
                (av_in, akv.at[0, pl.ds(2, 2)]),
                (bq_in, bq.at[h]),
                (aq_in, aq),
            ]
        )
    ]
    for copy in locals_:
        copy.start()
    own0, own1 = bt_in[0, 0], bt_in[0, 1]
    tlane = lax.broadcasted_iota(jnp.int32, (8, 128), 1)
    bt[0] = jnp.where(tlane == 0, own0, own1)

    @pl.when(core == 0)
    def _():
        pl.semaphore_wait(barrier, 3)

    @pl.when(core == 1)
    def _():
        pl.semaphore_wait(barrier, 2)

    def remote(src, dst, send, recv, target):
        return pltpu.make_async_remote_copy(
            src_ref=src, dst_ref=dst, send_sem=send, recv_sem=recv, device_id=target, device_id_type=MESH
        )

    def half_copy(slot, half, s_from, s_to, target):
        sems = (a_send, a_recv) if half is h else (b_send, b_recv)
        return remote(
            bkv.at[s_from, half], bkv.at[s_to, half], sems[0].at[slot], sems[1].at[s_to - 1], target
        )

    def a_copies(slot, s_from, s_to, target):
        return [
            half_copy(slot, h, s_from, s_to, target),
            remote(akv.at[s_from], akv.at[s_to], f_send.at[slot], f_recv.at[s_to - 1], target),
            remote(bt.at[s_from], bt.at[s_to], t_send.at[slot], t_recv.at[s_to - 1], target),
        ]

    def b_copies(slot, s_from, s_to, target):
        return [half_copy(slot, other, s_from, s_to, target)]

    near, far = at(e + 1, h), at(e + 2, h)
    partner = at(e, other)

    def start(copies):
        for copy in copies:
            copy.start()

    def first_sends(copies):
        start(copies(0, 0, 1, near))

    def forward_one(copies):
        @pl.when(core == 0)
        def _():
            start(copies(1, 1, 2, near))
            start(copies(2, 0, 2, far))
            start(copies(3, 1, 3, far))

    def forward_two(copies):
        @pl.when(core == 0)
        def _():
            start(copies(4, 2, 3, near))

    def wait_a(s):
        for copy in a_copies(0, s - 1, s, near):
            copy.wait_recv()

    def wait_b(s):
        for copy in b_copies(0, s - 1, s, near):
            copy.wait_recv()

    ex_kv = remote(bkv.at[0, h], bkv.at[0, h], ex_send.at[0], ex_recv.at[0], partner)
    ex_q = remote(bq.at[h], bq.at[h], ex_send.at[1], ex_recv.at[1], partner)
    for copy in locals_[:4]:
        copy.wait()
    ex_kv.start()
    first_sends(a_copies)
    locals_[4].wait()
    ex_q.start()
    locals_[5].wait()

    def scalars(s):
        copy = pltpu.make_async_copy(bt.at[s], bts.at[s], bts_sem.at[s])
        copy.start()
        copy.wait()
        b0, b1 = bts[s, 0, 0], bts[s, 0, 1]
        return (b0 > b1).astype(jnp.int32), jnp.minimum(b0, b1)

    def prep_a(s):
        x = akv[s].astype(F32)
        keys = x[0:2].reshape(32, 2 * HALF)
        keys_t = jnp.concatenate([keys, jnp.zeros((96, 2 * HALF), F32)], axis=0).T
        akt[s, 0] = keys_t[:HALF]
        akt[s, 1] = keys_t[HALF:]
        avj[s, 0] = x[2:4, :, :HALF]
        avj[s, 1] = x[2:4, :, HALF:]

    def prep_b(s, j):
        bkf[s, j] = bkv[s, j, 0].astype(F32)
        v = bkv[s, j, 1].astype(F32)
        v = jnp.concatenate([v, jnp.zeros((64, 2 * DH), F32)], axis=0).T
        bvt[s, j] = v[:, :HALF]

    def prep_q(j):
        b = bq[j].astype(F32)
        bqt[j] = jnp.concatenate([b, b], axis=0).T.astype(BF16)

    def prep_aq():
        x = aq[...].astype(F32)
        low, high = x[:, :PAIRS], x[:, PAIRS:]
        wide = first[None]

        def turned(y):
            return pltpu.roll(y.reshape(RQ * PAIRS, 2 * HALF), HALF, 1).reshape(y.shape)

        a2q[0] = jnp.where(wide, low, turned(high))
        a2q[1] = jnp.where(wide, turned(low), high)

    def build_q(j, p):
        total = a2q[j, 0, pl.ds(p, 1), :] * bqt[j, 0:DH, :].astype(F32)
        for r in range(1, RQ):
            total += a2q[j, r, pl.ds(p, 1), :] * bqt[j, r * DH : (r + 1) * DH, :].astype(F32)
        total = total * (1.0 / RQ)
        qbd[j, p, 0:DH] = jnp.where(first, total, 0.0).astype(BF16)
        qbd[j, p, DH : 2 * DH] = jnp.where(first, 0.0, total).astype(BF16)

    def build_kv(s, j, p):
        a = pltpu.roll(akt[s, j], lax.rem(128 - p, 128), 1)
        b0, b1 = bkf[s, j, :, 0:DH], bkf[s, j, :, DH : 2 * DH]
        ka = a[:, 0:1] * b0 + a[:, 16:17] * b1
        kb = a[:, 8:9] * b0 + a[:, 24:25] * b1
        keys = jnp.concatenate([ka.astype(BF16), kb.astype(BF16)], axis=1)
        c0, c1 = bvt[s, j, 0:DH], bvt[s, j, DH : 2 * DH]
        va = avj[s, j, 0, pl.ds(p, 1), :] * c0 + avj[s, j, 1, pl.ds(p, 1), :] * c1
        vb = avj[s, j, 0, pl.ds(p + PAIRS, 1), :] * c0 + avj[s, j, 1, pl.ds(p + PAIRS, 1), :] * c1
        values = jnp.concatenate([va.astype(BF16), vb.astype(BF16)], axis=0)
        return keys, values

    def dot(x, y):
        return jnp.dot(x, y, preferred_element_type=F32)

    def weigh(scores, top, values):
        weights = jnp.exp2((scores - top) * SCALE2)
        total = jnp.sum(weights, axis=0, keepdims=True)
        both = dot(values, weights.astype(BF16))
        return total, jnp.where(first, both[:DH], both[DH:])

    def highest(scores):
        return jnp.max(scores, axis=0, keepdims=True)

    def merge(state, scores, values):
        m, l, o = state
        top = jnp.maximum(m, highest(scores))
        total, added = weigh(scores, top, values)
        rescale = jnp.exp2((m - top) * SCALE2)
        return top, l * rescale + total, o * rescale + added

    def diagonal(j, p):
        keys, values = build_kv(0, j, p)
        scores = dot(keys, qbd[j, p])
        row = lax.broadcasted_iota(jnp.int32, scores.shape, 0)
        col = lax.broadcasted_iota(jnp.int32, scores.shape, 1)
        col = jnp.where(col < HALF, col, col - HALF)
        scores = jnp.where(row <= col, scores, MASKED)
        top = highest(scores)
        total, added = weigh(scores, top, values)
        m_own[j, p] = top
        l_own[j, p] = total
        o_own[j, p] = added

    def each_pair(body):
        def step(p, carry):
            body(p)
            return carry

        lax.fori_loop(0, PAIRS, step, 0)

    jl0, low0 = scalars(0)
    prep_aq()
    prep_a(0)
    prep_q(h)
    prep_b(0, h)

    def own_half(p):
        build_q(h, p)
        diagonal(h, p)

    each_pair(own_half)

    ex_kv.wait_recv()
    first_sends(b_copies)
    wait_a(1)
    forward_one(a_copies)
    prep_b(0, other)
    ex_q.wait_recv()
    prep_q(other)

    def other_half(p):
        build_q(other, p)
        diagonal(other, p)

    each_pair(other_half)
    wait_b(1)
    forward_one(b_copies)

    def low_keys(p):
        keys, values = build_kv(0, jl0, p)
        scores = dot(keys, qbd[1 - jl0, p])
        m, l, o = merge((m_own[1 - jl0, p], l_own[1 - jl0, p], o_own[1 - jl0, p]), scores, values)
        m_acc[1, p], l_acc[1, p], o_acc[1, p] = m, l, o
        m_acc[0, p], l_acc[0, p], o_acc[0, p] = m_own[jl0, p], l_own[jl0, p], o_own[jl0, p]

    each_pair(low_keys)

    for s in range(1, 4):
        if s > 1:
            wait_a(s)
            if s == 2:
                forward_two(a_copies)
            wait_b(s)
            if s == 2:
                forward_two(b_copies)
        jls, lows = scalars(s)
        pick = (lows > low0).astype(jnp.int32)
        jq = jl0 + pick - 2 * jl0 * pick
        jk = jls + pick - 2 * jls * pick
        prep_a(s)
        prep_b(s, 0)
        prep_b(s, 1)

        def one_offset(p):
            keys, values = build_kv(s, jls, p)
            scores = dot(keys, qbd[1 - jl0, p])
            keys2, values2 = build_kv(s, jk, p)
            scores2 = dot(keys2, qbd[jq, p])
            high = merge((m_acc[1, p], l_acc[1, p], o_acc[1, p]), scores, values)
            low = (m_acc[0, p], l_acc[0, p], o_acc[0, p])
            is_high = pick == 1
            old = tuple(jnp.where(is_high, x, y) for x, y in zip(high, low))
            new = merge(old, scores2, values2)
            m_acc[1, p], l_acc[1, p], o_acc[1, p] = (jnp.where(is_high, x, y) for x, y in zip(new, high))
            m_acc[0, p], l_acc[0, p], o_acc[0, p] = (jnp.where(is_high, x, y) for x, y in zip(low, new))

        each_pair(one_offset)

    def finish(p):
        for j in range(2):
            k = jl0 if j == 0 else 1 - jl0
            m, l, o = m_acc[k, p], l_acc[k, p], o_acc[k, p]
            rows = (o * (0.5 / l)).T.astype(BF16)
            out_ref[p, j * HALF : (j + 1) * HALF, :] = rows[:HALF]
            out_ref[p + PAIRS, j * HALF : (j + 1) * HALF, :] = rows[HALF:]
            logs[j, pl.ds(p, 1), :] = m * SCALE + jnp.log(l)

    each_pair(finish)
    log0, log1 = logs[0], logs[1]
    log_ref[0:PAIRS] = jnp.where(first, log0, pltpu.roll(log1, HALF, 1))
    log_ref[PAIRS:] = jnp.where(first, pltpu.roll(log0, HALF, 1), log1)

    ex_kv.wait_send()
    ex_q.wait_send()
    for copies in (a_copies, b_copies):
        for copy in copies(0, 0, 1, near):
            copy.wait_send()

    @pl.when(core == 0)
    def _():
        for copies in (a_copies, b_copies):
            for slot in range(1, 5):
                for copy in copies(slot, 0, 1, near):
                    copy.wait_send()


def on_device(block_table, a_query, b_query, a_key, b_key, a_value, b_value):
    rows = 2 * HALF
    heads = 2 * PAIRS
    hbm = pl.BlockSpec(memory_space=pl.ANY)
    vmem = pl.BlockSpec(memory_space=pltpu.VMEM)
    dma = pltpu.SemaphoreType.DMA
    return pl.pallas_call(
        kernel,
        out_shape=(
            jax.ShapeDtypeStruct((heads, rows, DH), BF16),
            jax.ShapeDtypeStruct((heads, rows), F32),
        ),
        in_specs=[pl.BlockSpec(memory_space=pltpu.SMEM)] + [hbm] * 6,
        out_specs=(vmem, vmem),
        scratch_shapes=[
            pltpu.VMEM((4, 8, 128), jnp.int32),
            pltpu.SMEM((4, 8, 128), jnp.int32),
            pltpu.VMEM((RQ, heads, rows), BF16),
            pltpu.VMEM((2, HALF, RQ * DH), BF16),
            pltpu.VMEM((4, 2, 2, HALF, 2 * DH), BF16),
            pltpu.VMEM((4, 4, heads, rows), BF16),
            pltpu.VMEM((2, RQ * DH, rows), BF16),
            pltpu.VMEM((2, RQ, PAIRS, rows), F32),
            pltpu.VMEM((2, PAIRS, 2 * DH, rows), BF16),
            pltpu.VMEM((4, 2, HALF, 2 * DH), F32),
            pltpu.VMEM((4, 2, 2 * DH, HALF), F32),
            pltpu.VMEM((4, 2, HALF, 128), F32),
            pltpu.VMEM((4, 2, 2, heads, HALF), F32),
            pltpu.VMEM((2, PAIRS, DH, rows), F32),
            pltpu.VMEM((2, PAIRS, 1, rows), F32),
            pltpu.VMEM((2, PAIRS, 1, rows), F32),
            pltpu.VMEM((2, PAIRS, DH, rows), F32),
            pltpu.VMEM((2, PAIRS, 1, rows), F32),
            pltpu.VMEM((2, PAIRS, 1, rows), F32),
            pltpu.VMEM((2, PAIRS, rows), F32),
            dma((6,)),
            dma((4,)),
            dma((2,)),
            dma((2,)),
            dma((5,)),
            dma((3,)),
            dma((5,)),
            dma((3,)),
            dma((5,)),
            dma((3,)),
            dma((5,)),
            dma((3,)),
        ],
        compiler_params=pltpu.CompilerParams(
            collective_id=0, has_side_effects=True, vmem_limit_bytes=48 * 1024 * 1024
        ),
    )(block_table, a_query, b_query, a_key, b_key, a_value, b_value)


def solution(mesh):
    in_specs = (
        P("blk", None),
        P(None, "head", "blk"),
        P(("blk", "head"), None),
        P(None, "head", "blk"),
        P(("blk", "head"), None),
        P(None, "head", "blk"),
        P(("blk", "head"), None),
    )
    out_specs = (P("head", "blk", None), P("head", "blk"))
    return jax.shard_map(
        on_device, mesh=mesh, in_specs=in_specs, out_specs=out_specs, check_vma=False
    )
```

time: 212 us -> 67 us (0.32)
  the two profiles are of different devices: /device:TPU:24 before, /device:TPU:8 now
where the time goes in v1:
time: 67 us; the launch traced here: 66.6 us
  Pallas kernels  58.4 us (87%)
  local copies, waits for them, and re-layouts  7.5 us (11%)
    pallas_call x1, Pallas kernels, on_device(): pl.pallas_call(kernel, out_shape=(jax.ShapeDtypeStruct((heads, rows, DH),...  58.4 us
    unnamed x16, local copies, waits for them, and re-layouts  7.5 us

profile of v1, /device:TPU:8, one launch (start us, length us, event | category | flops | bytes accessed | tf_op | source)
XLA Modules:
  0.0 66.6 jit_solution(1167426358021486677)
XLA Ops:
  0.6 0.0 copy-start
  0.6 1.0 %copy-done = bf16[192,768]{1,0:T(8,128)(2,1)S(1)} copy-done((bf16[192,768]{1,0:T(8,128)(2,1)S(1)}, bf16[192,768]{1,0:T(8,128)(2,1)}, u32[]{:S(2)}) %copy-start) | copy-done | bytes 294936
  1.6 0.0 copy-start.1
  1.6 0.9 %copy-done.1 = bf16[192,256]{1,0:T(8,128)(2,1)S(1)} copy-done((bf16[192,256]{1,0:T(8,128)(2,1)S(1)}, bf16[192,256]{1,0:T(8,128)(2,1)}, u32[]{:S(2)}) %copy-start.1) | copy-done | bytes 98328
  2.5 0.0 copy-start.2
  2.5 0.9 %copy-done.2 = bf16[192,256]{1,0:T(8,128)(2,1)S(1)} copy-done((bf16[192,256]{1,0:T(8,128)(2,1)S(1)}, bf16[192,256]{1,0:T(8,128)(2,1)}, u32[]{:S(2)}) %copy-start.2) | copy-done | bytes 98328
  3.4 0.0 copy-start.3
  3.4 0.9 %copy-done.3 = bf16[6,16,384]{2,1,0:T(8,128)(2,1)S(1)} copy-done((bf16[6,16,384]{2,1,0:T(8,128)(2,1)S(1)}, bf16[6,16,384]{2,1,0:T(8,128)(2,1)}, u32[]{:S(2)}) %copy-start.3) | copy-done | bytes 73752
  4.3 0.0 copy-start.4
  4.3 0.7 %copy-done.4 = bf16[2,16,384]{2,1,0:T(8,128)(2,1)S(1)} copy-done((bf16[2,16,384]{2,1,0:T(8,128)(2,1)S(1)}, bf16[2,16,384]{2,1,0:T(8,128)(2,1)}, u32[]{:S(2)}) %copy-start.4) | copy-done | bytes 24600
  5.0 0.0 copy-start.5
  5.0 0.7 %copy-done.5 = bf16[2,16,384]{2,1,0:T(8,128)(2,1)S(1)} copy-done((bf16[2,16,384]{2,1,0:T(8,128)(2,1)S(1)}, bf16[2,16,384]{2,1,0:T(8,128)(2,1)}, u32[]{:S(2)}) %copy-start.5) | copy-done | bytes 24600
  5.7 0.0 copy-start.6
  5.7 0.7 copy-done.6
  6.4 58.4 %shard_map.86 = (bf16[16,384,128]{2,1,0:T(8,128)(2,1)S(1)}, f32[16,384]{1,0:T(8,128)S(1)}) custom-call(s32[1,2]{1,0:T(1,128)S(1)} %copy-done.6, bf16[6,16,384]{2,1,0:T(8,128)(2,1)S(1)} %copy-done.3, bf16[192,768]{1,0:T(8,128)(2,1)S(1)} %copy-done, bf16[2,16,384]{2,1,0:T(8,128)(2,1)S(1)} %copy-done.4, bf16[192,256]{1,0:T(8,128)(2,1)S(1)} %copy-done.1, ...), custom_call_target="tpu_custom_call" | custom-call | tf_op jit(solution)/shard_map/pallas_call | solution.py:335
  64.8 1.1 %copy.11 = bf16[16,384,128]{2,1,0:T(8,128)(2,1)} copy(bf16[16,384,128]{2,1,0:T(8,128)(2,1)S(1)} %get-tuple-element.4) | data formatting | bytes 3145728
  66.0 0.6 copy.12
Async XLA Ops:
  0.6 1.0 %copy-start = (bf16[192,768]{1,0:T(8,128)(2,1)S(1)}, bf16[192,768]{1,0:T(8,128)(2,1)}, u32[]{:S(2)}) copy-start(bf16[192,768]{1,0:T(8,128)(2,1)} %bq_in.1) | copy-start | bytes 884740
  1.6 0.9 %copy-start.1 = (bf16[192,256]{1,0:T(8,128)(2,1)S(1)}, bf16[192,256]{1,0:T(8,128)(2,1)}, u32[]{:S(2)}) copy-start(bf16[192,256]{1,0:T(8,128)(2,1)} %bk_in.1) | copy-start | bytes 294916
  2.5 0.9 %copy-start.2 = (bf16[192,256]{1,0:T(8,128)(2,1)S(1)}, bf16[192,256]{1,0:T(8,128)(2,1)}, u32[]{:S(2)}) copy-start(bf16[192,256]{1,0:T(8,128)(2,1)} %bv_in.1) | copy-start | bytes 294916
  3.4 0.9 %copy-start.3 = (bf16[6,16,384]{2,1,0:T(8,128)(2,1)S(1)}, bf16[6,16,384]{2,1,0:T(8,128)(2,1)}, u32[]{:S(2)}) copy-start(bf16[6,16,384]{2,1,0:T(8,128)(2,1)} %aq_in.1) | copy-start | bytes 221188
  4.3 0.7 %copy-start.4 = (bf16[2,16,384]{2,1,0:T(8,128)(2,1)S(1)}, bf16[2,16,384]{2,1,0:T(8,128)(2,1)}, u32[]{:S(2)}) copy-start(bf16[2,16,384]{2,1,0:T(8,128)(2,1)} %ak_in.1) | copy-start | bytes 73732
  5.0 0.7 %copy-start.5 = (bf16[2,16,384]{2,1,0:T(8,128)(2,1)S(1)}, bf16[2,16,384]{2,1,0:T(8,128)(2,1)}, u32[]{:S(2)}) copy-start(bf16[2,16,384]{2,1,0:T(8,128)(2,1)} %av_in.1) | copy-start | bytes 73732
  5.7 0.7 copy-start.6

commit v2 on v1

--- a/solution.py
+++ b/solution.py
@@ -15,17 +15,16 @@
 F32 = jnp.float32
 BF16 = jnp.bfloat16
 SCALE = 0.5 / math.sqrt(DH)
-SCALE2 = SCALE * math.log2(math.e)
 MASKED = -1e30
 
 
 def kernel(
     bt_in, aq_in, bq_in, ak_in, bk_in, av_in, bv_in,
-    out_ref, log_ref,
-    bt, bts, aq, bq, bkv, akv,
-    bqt, a2q, qbd, bkf, bvt, akt, avj,
-    o_own, m_own, l_own, o_acc, m_acc, l_acc, logs,
-    local_sem, bts_sem, ex_send, ex_recv, a_send, a_recv, f_send, f_recv, t_send, t_recv, b_send, b_recv,
+    out_hbm, log_hbm,
+    out_ref, log_ref, bt, bts, aq, bq, bkv, akv,
+    bqt, a2q, qbd, bkf, bvt, akt, avj, kb, vb,
+    o_acc, m_acc, l_acc, logs,
+    out_sem, local_sem, bts_sem, ex_send, ex_recv, a_send, a_recv, f_send, f_recv, t_send, t_recv, b_send, b_recv,
 ):
     e = lax.axis_index("blk")
     h = lax.axis_index("head")
@@ -183,134 +182,172 @@
         a = pltpu.roll(akt[s, j], lax.rem(128 - p, 128), 1)
         b0, b1 = bkf[s, j, :, 0:DH], bkf[s, j, :, DH : 2 * DH]
         ka = a[:, 0:1] * b0 + a[:, 16:17] * b1
-        kb = a[:, 8:9] * b0 + a[:, 24:25] * b1
-        keys = jnp.concatenate([ka.astype(BF16), kb.astype(BF16)], axis=1)
+        kb_ = a[:, 8:9] * b0 + a[:, 24:25] * b1
         c0, c1 = bvt[s, j, 0:DH], bvt[s, j, DH : 2 * DH]
         va = avj[s, j, 0, pl.ds(p, 1), :] * c0 + avj[s, j, 1, pl.ds(p, 1), :] * c1
-        vb = avj[s, j, 0, pl.ds(p + PAIRS, 1), :] * c0 + avj[s, j, 1, pl.ds(p + PAIRS, 1), :] * c1
-        values = jnp.concatenate([va.astype(BF16), vb.astype(BF16)], axis=0)
-        return keys, values
+        vb_ = avj[s, j, 0, pl.ds(p + PAIRS, 1), :] * c0 + avj[s, j, 1, pl.ds(p + PAIRS, 1), :] * c1
+        kb[s, j, p, :, 0:DH] = ka.astype(BF16)
+        kb[s, j, p, :, DH : 2 * DH] = kb_.astype(BF16)
+        vb[s, j, p, 0:DH] = va.astype(BF16)
+        vb[s, j, p, DH : 2 * DH] = vb_.astype(BF16)
 
     def dot(x, y):
         return jnp.dot(x, y, preferred_element_type=F32)
 
+    middle = lax.broadcasted_iota(jnp.int32, (1, DH), 1) < HALF - DH
+
     def weigh(scores, top, values):
-        weights = jnp.exp2((scores - top) * SCALE2)
+        weights = jnp.exp((scores - top) * SCALE)
         total = jnp.sum(weights, axis=0, keepdims=True)
-        both = dot(values, weights.astype(BF16))
-        return total, jnp.where(first, both[:DH], both[DH:])
+        rounded = weights.astype(BF16)
+        both = dot(values, rounded[:, : 2 * DH])
+        last = dot(values[DH:], rounded[:, 2 * DH :])
+        out = jnp.concatenate(
+            [both[:DH, :DH], jnp.where(middle, both[:DH, DH:], both[DH:, DH:]), last], axis=1
+        )
+        return total, out
 
     def highest(scores):
         return jnp.max(scores, axis=0, keepdims=True)
 
-    def merge(state, scores, values):
-        m, l, o = state
-        top = jnp.maximum(m, highest(scores))
-        total, added = weigh(scores, top, values)
-        rescale = jnp.exp2((m - top) * SCALE2)
-        return top, l * rescale + total, o * rescale + added
-
-    def diagonal(j, p):
-        keys, values = build_kv(0, j, p)
-        scores = dot(keys, qbd[j, p])
-        row = lax.broadcasted_iota(jnp.int32, scores.shape, 0)
-        col = lax.broadcasted_iota(jnp.int32, scores.shape, 1)
-        col = jnp.where(col < HALF, col, col - HALF)
-        scores = jnp.where(row <= col, scores, MASKED)
-        top = highest(scores)
-        total, added = weigh(scores, top, values)
-        m_own[j, p] = top
-        l_own[j, p] = total
-        o_own[j, p] = added
-
-    def each_pair(body):
+    def loop(body, both):
         def step(p, carry):
-            body(p)
+            if both:
+                done = [body(p), body(p + PAIRS // 2)]
+            else:
+                done = [body(p)]
+            for store in done:
+                if store is not None:
+                    store()
             return carry
 
-        lax.fori_loop(0, PAIRS, step, 0)
-
-    jl0, low0 = scalars(0)
-    prep_aq()
-    prep_a(0)
-    prep_q(h)
-    prep_b(0, h)
-
-    def own_half(p):
-        build_q(h, p)
-        diagonal(h, p)
-
-    each_pair(own_half)
-
-    ex_kv.wait_recv()
-    first_sends(b_copies)
-    wait_a(1)
-    forward_one(a_copies)
-    prep_b(0, other)
-    ex_q.wait_recv()
-    prep_q(other)
-
-    def other_half(p):
-        build_q(other, p)
-        diagonal(other, p)
-
-    each_pair(other_half)
-    wait_b(1)
-    forward_one(b_copies)
-
-    def low_keys(p):
-        keys, values = build_kv(0, jl0, p)
-        scores = dot(keys, qbd[1 - jl0, p])
-        m, l, o = merge((m_own[1 - jl0, p], l_own[1 - jl0, p], o_own[1 - jl0, p]), scores, values)
-        m_acc[1, p], l_acc[1, p], o_acc[1, p] = m, l, o
-        m_acc[0, p], l_acc[0, p], o_acc[0, p] = m_own[jl0, p], l_own[jl0, p], o_own[jl0, p]
-
-    each_pair(low_keys)
-
-    for s in range(1, 4):
-        if s > 1:
-            wait_a(s)
-            if s == 2:
-                forward_two(a_copies)
-            wait_b(s)
-            if s == 2:
-                forward_two(b_copies)
+        lax.fori_loop(0, PAIRS // 2 if both else PAIRS, step, 0)
+
+    def build_half(s, j):
+        prep_b(s, j)
+        loop(lambda p: build_kv(s, j, p), False)
+
+    def put(which, p, state):
+        m_acc[which, p], l_acc[which, p], o_acc[which, p] = state
+
+    def get(which, p):
+        return m_acc[which, p], l_acc[which, p], o_acc[which, p]
+
+    def own_position(p):
+        k_low, v_low = kb[0, jl0, p], vb[0, jl0, p]
+        k_high, v_high = kb[0, 1 - jl0, p], vb[0, 1 - jl0, p]
+        q_low, q_high = qbd[jl0, p], qbd[1 - jl0, p]
+        shape = (HALF, 2 * HALF)
+        row = lax.broadcasted_iota(jnp.int32, shape, 0)
+        col = lax.broadcasted_iota(jnp.int32, shape, 1)
+        seen = row <= jnp.where(col < HALF, col, col - HALF)
+        low = jnp.where(seen, dot(k_low, q_low), MASKED)
+        cross = dot(k_low, q_high)
+        high = jnp.where(seen, dot(k_high, q_high), MASKED)
+        m_low = highest(low)
+        m_high = jnp.maximum(highest(cross), highest(high))
+        l_low, o_low = weigh(low, m_low, v_low)
+        l_cross, o_cross = weigh(cross, m_high, v_low)
+        l_high, o_high = weigh(high, m_high, v_high)
+
+        def store():
+            put(0, p, (m_low, l_low, o_low))
+            put(1, p, (m_high, l_cross + l_high, o_cross + o_high))
+
+        return store
+
+    def earlier_position(s, last=False):
         jls, lows = scalars(s)
         pick = (lows > low0).astype(jnp.int32)
         jq = jl0 + pick - 2 * jl0 * pick
         jk = jls + pick - 2 * jls * pick
-        prep_a(s)
-        prep_b(s, 0)
-        prep_b(s, 1)
-
-        def one_offset(p):
-            keys, values = build_kv(s, jls, p)
-            scores = dot(keys, qbd[1 - jl0, p])
-            keys2, values2 = build_kv(s, jk, p)
-            scores2 = dot(keys2, qbd[jq, p])
-            high = merge((m_acc[1, p], l_acc[1, p], o_acc[1, p]), scores, values)
-            low = (m_acc[0, p], l_acc[0, p], o_acc[0, p])
-            is_high = pick == 1
-            old = tuple(jnp.where(is_high, x, y) for x, y in zip(high, low))
-            new = merge(old, scores2, values2)
-            m_acc[1, p], l_acc[1, p], o_acc[1, p] = (jnp.where(is_high, x, y) for x, y in zip(new, high))
-            m_acc[0, p], l_acc[0, p], o_acc[0, p] = (jnp.where(is_high, x, y) for x, y in zip(low, new))
-
-        each_pair(one_offset)
-
-    def finish(p):
-        for j in range(2):
-            k = jl0 if j == 0 else 1 - jl0
-            m, l, o = m_acc[k, p], l_acc[k, p], o_acc[k, p]
-            rows = (o * (0.5 / l)).T.astype(BF16)
-            out_ref[p, j * HALF : (j + 1) * HALF, :] = rows[:HALF]
-            out_ref[p + PAIRS, j * HALF : (j + 1) * HALF, :] = rows[HALF:]
-            logs[j, pl.ds(p, 1), :] = m * SCALE + jnp.log(l)
-
-    each_pair(finish)
+        is_high = pick == 1
+
+        def body(p):
+            m_low, l_low, o_low = get(0, p)
+            m_high, l_high, o_high = get(1, p)
+            k1, v1, q1 = kb[s, jls, p], vb[s, jls, p], qbd[1 - jl0, p]
+            k2, v2, q2 = kb[s, jk, p], vb[s, jk, p], qbd[jq, p]
+            s1 = dot(k1, q1)
+            s2 = dot(k2, q2)
+            top1, top2 = highest(s1), highest(s2)
+            high = jnp.maximum(jnp.maximum(m_high, top1), jnp.where(is_high, top2, MASKED))
+            low = jnp.maximum(m_low, jnp.where(is_high, MASKED, top2))
+            t1, o1 = weigh(s1, high, v1)
+            t2, o2 = weigh(s2, jnp.where(is_high, high, low), v2)
+            r_high = jnp.exp((m_high - high) * SCALE)
+            r_low = jnp.exp((m_low - low) * SCALE)
+            l_high = l_high * r_high + t1 + jnp.where(is_high, t2, 0.0)
+            l_low = l_low * r_low + jnp.where(is_high, 0.0, t2)
+            o_high = o_high * r_high + o1 + jnp.where(is_high, o2, 0.0)
+            o_low = o_low * r_low + jnp.where(is_high, 0.0, o2)
+
+            def store():
+                if not last:
+                    put(0, p, (low, l_low, o_low))
+                    put(1, p, (high, l_high, o_high))
+                    return
+                rows_low = (o_low * (0.5 / l_low)).T.astype(BF16)
+                rows_high = (o_high * (0.5 / l_high)).T.astype(BF16)
+                log_low = low * SCALE + jnp.log(l_low)
+                log_high = high * SCALE + jnp.log(l_high)
+                for j in range(2):
+                    is_low = jl0 == j
+                    rows = jnp.where(is_low, rows_low, rows_high)
+                    out_ref[p, j * HALF : (j + 1) * HALF, :] = rows[:HALF]
+                    out_ref[p + PAIRS, j * HALF : (j + 1) * HALF, :] = rows[HALF:]
+                    logs[j, pl.ds(p, 1), :] = jnp.where(is_low, log_low, log_high)
+                for head in (p, p + PAIRS):
+                    write_out(head).start()
+
+            return store
+
+        loop(body, True)
+
+    def write_out(head):
+        return pltpu.make_async_copy(out_ref.at[head], out_hbm.at[head], out_sem.at[head])
+
+    jl0, low0 = scalars(0)
+    prep_a(0)
+    build_half(0, h)
+    prep_aq()
+    prep_q(h)
+    ex_kv.wait_recv()
+    first_sends(b_copies)
+    loop(lambda p: build_q(h, p), False)
+    wait_a(1)
+    forward_one(a_copies)
+    build_half(0, other)
+    prep_a(1)
+    build_half(1, h)
+    wait_b(1)
+    forward_one(b_copies)
+    build_half(1, other)
+    wait_a(2)
+    forward_two(a_copies)
+    prep_a(2)
+    build_half(2, h)
+    ex_q.wait_recv()
+    prep_q(other)
+    loop(lambda p: build_q(other, p), False)
+    loop(own_position, True)
+    wait_b(2)
+    forward_two(b_copies)
+    earlier_position(1)
+    build_half(2, other)
+    earlier_position(2)
+    wait_a(3)
+    prep_a(3)
+    build_half(3, h)
+    wait_b(3)
+    build_half(3, other)
+    earlier_position(3, last=True)
     log0, log1 = logs[0], logs[1]
     log_ref[0:PAIRS] = jnp.where(first, log0, pltpu.roll(log1, HALF, 1))
     log_ref[PAIRS:] = jnp.where(first, pltpu.roll(log0, HALF, 1), log1)
+
+    write_log = pltpu.make_async_copy(log_ref, log_hbm, out_sem.at[2 * PAIRS])
+    write_log.start()
 
     ex_kv.wait_send()
     ex_q.wait_send()
@@ -325,12 +362,15 @@
                 for copy in copies(slot, 0, 1, near):
                     copy.wait_send()
 
+    for head in range(2 * PAIRS):
+        write_out(head).wait()
+    write_log.wait()
+
 
 def on_device(block_table, a_query, b_query, a_key, b_key, a_value, b_value):
     rows = 2 * HALF
     heads = 2 * PAIRS
-    hbm = pl.BlockSpec(memory_space=pl.ANY)
-    vmem = pl.BlockSpec(memory_space=pltpu.VMEM)
+    hbm = pl.BlockSpec(memory_space=pltpu.HBM)
     dma = pltpu.SemaphoreType.DMA
     return pl.pallas_call(
         kernel,
@@ -339,8 +379,10 @@
             jax.ShapeDtypeStruct((heads, rows), F32),
         ),
         in_specs=[pl.BlockSpec(memory_space=pltpu.SMEM)] + [hbm] * 6,
-        out_specs=(vmem, vmem),
+        out_specs=(hbm, hbm),
         scratch_shapes=[
+            pltpu.VMEM((heads, rows, DH), BF16),
+            pltpu.VMEM((heads, rows), F32),
             pltpu.VMEM((4, 8, 128), jnp.int32),
             pltpu.SMEM((4, 8, 128), jnp.int32),
             pltpu.VMEM((RQ, heads, rows), BF16),
@@ -354,13 +396,13 @@
             pltpu.VMEM((4, 2, 2 * DH, HALF), F32),
             pltpu.VMEM((4, 2, HALF, 128), F32),
             pltpu.VMEM((4, 2, 2, heads, HALF), F32),
-            pltpu.VMEM((2, PAIRS, DH, rows), F32),
-            pltpu.VMEM((2, PAIRS, 1, rows), F32),
-            pltpu.VMEM((2, PAIRS, 1, rows), F32),
+            pltpu.VMEM((4, 2, PAIRS, HALF, 2 * DH), BF16),
+            pltpu.VMEM((4, 2, PAIRS, 2 * DH, HALF), BF16),
             pltpu.VMEM((2, PAIRS, DH, rows), F32),
             pltpu.VMEM((2, PAIRS, 1, rows), F32),
             pltpu.VMEM((2, PAIRS, 1, rows), F32),
             pltpu.VMEM((2, PAIRS, rows), F32),
+            dma((heads + 1,)),
             dma((6,)),
             dma((4,)),
             dma((2,)),
@@ -375,7 +417,7 @@
             dma((3,)),
         ],
         compiler_params=pltpu.CompilerParams(
-            collective_id=0, has_side_effects=True, vmem_limit_bytes=48 * 1024 * 1024
+            collective_id=0, has_side_effects=True, vmem_limit_bytes=60 * 1024 * 1024
         ),
     )(block_table, a_query, b_query, a_key, b_key, a_value, b_value)
 

time: 67 us -> 63.4 us (0.946)
  the two profiles are of different devices: /device:TPU:8 before, /device:TPU:24 now
where the time goes in v2:
time: 63.4 us; the launch traced here: 62.7 us
  Pallas kernels  58.7 us (93%)
  local copies, waits for them, and re-layouts  3.32 us (5%)
  between operations  0.65 us (1%)
    pallas_call x1, Pallas kernels, on_device(): pl.pallas_call(kernel, out_shape=(jax.ShapeDtypeStruct((heads, rows, DH),...  58.7 us
    unnamed x4, local copies, waits for them, and re-layouts  3.32 us

profile of v2, /device:TPU:24, one launch (start us, length us, event | category | flops | bytes accessed | tf_op | source)
XLA Modules:
  0.0 62.7 jit_solution(14556594414547628103)
XLA Ops:
  0.6 58.7 %shard_map.86 = (bf16[16,384,128]{2,1,0:T(8,128)(2,1)}, f32[16,384]{1,0:T(8,128)}) custom-call(s32[1,2]{1,0:T(1,128)} %bt_in.1, bf16[6,16,384]{2,1,0:T(8,128)(2,1)} %aq_in.1, bf16[192,768]{1,0:T(8,128)(2,1)} %bq_in.1, bf16[2,16,384]{2,1,0:T(8,128)(2,1)} %ak_in.1, bf16[192,256]{1,0:T(8,128)(2,1)} %bk_in.1, bf16[2,16,384]{2,1,0:T(8,128)(2,1)} %av_in.1, ...), custom_call_target="tpu_custom_call" | custom-call | tf_op jit(solution)/shard_map/pallas_call | solution.py:375
  59.4 0.0 copy-start
  59.4 2.7 %copy.11 = bf16[16,384,128]{2,1,0:T(8,128)(2,1)} copy(bf16[16,384,128]{2,1,0:T(8,128)(2,1)} %get-tuple-element.4) | data formatting | bytes 3145728
  62.1 0.0 copy-done
  62.1 0.6 copy.12
Async XLA Ops:
  59.4 2.7 %copy-start = (f32[16,384]{1,0:T(8,128)S(1)}, f32[16,384]{1,0:T(8,128)}, u32[]{:S(2)}) copy-start(f32[16,384]{1,0:T(8,128)} %get-tuple-element.5) | copy-start | bytes 73732

commit v3 on v2

--- a/solution.py
+++ b/solution.py
@@ -21,7 +21,7 @@
 def kernel(
     bt_in, aq_in, bq_in, ak_in, bk_in, av_in, bv_in,
     out_hbm, log_hbm,
-    out_ref, log_ref, bt, bts, aq, bq, bkv, akv,
+    relay_kv, relay_q, out_ref, log_ref, bt, bts, aq, bq, bkv, akv,
     bqt, a2q, qbd, bkf, bvt, akt, avj, kb, vb,
     o_acc, m_acc, l_acc, logs,
     out_sem, local_sem, bts_sem, ex_send, ex_recv, a_send, a_recv, f_send, f_recv, t_send, t_recv, b_send, b_recv,
@@ -37,13 +37,28 @@
     def at(blk, head):
         return {"blk": lax.rem(blk + places, places), "head": head}
 
+    across = e + places // 2
+    chip = lax.rem(e // 2, places // 4)
+    leaves = chip == places // 4 - 1
+    enters = jnp.logical_and(chip == 0, core == 0)
+
     barrier = pltpu.get_barrier_semaphore()
-    pl.semaphore_signal(barrier, inc=1, device_id=at(e - 1, h), device_id_type=MESH)
-    pl.semaphore_signal(barrier, inc=1, device_id=at(e, other), device_id_type=MESH)
+
+    def greet(target):
+        pl.semaphore_signal(barrier, inc=1, device_id=target, device_id_type=MESH)
+
+    greet(at(across, h))
+    greet(at(across, other))
+    greet(at(e - 1, h))
 
     @pl.when(core == 0)
     def _():
-        pl.semaphore_signal(barrier, inc=1, device_id=at(e - 2, h), device_id_type=MESH)
+        greet(at(e - 2, h))
+
+    @pl.when(enters)
+    def _():
+        greet(at(e - 1, other))
+        greet(at(e - 2, other))
 
     locals_ = [
         pltpu.make_async_copy(src, dst, local_sem.at[i])
@@ -64,38 +79,31 @@
     tlane = lax.broadcasted_iota(jnp.int32, (8, 128), 1)
     bt[0] = jnp.where(tlane == 0, own0, own1)
 
-    @pl.when(core == 0)
-    def _():
-        pl.semaphore_wait(barrier, 3)
-
-    @pl.when(core == 1)
-    def _():
-        pl.semaphore_wait(barrier, 2)
+    pl.semaphore_wait(barrier, 4 - core + leaves.astype(jnp.int32))
 
     def remote(src, dst, send, recv, target):
         return pltpu.make_async_remote_copy(
             src_ref=src, dst_ref=dst, send_sem=send, recv_sem=recv, device_id=target, device_id_type=MESH
         )
 
-    def half_copy(slot, half, s_from, s_to, target):
-        sems = (a_send, a_recv) if half is h else (b_send, b_recv)
-        return remote(
-            bkv.at[s_from, half], bkv.at[s_to, half], sems[0].at[slot], sems[1].at[s_to - 1], target
-        )
-
     def a_copies(slot, s_from, s_to, target):
+        to = target[0]
         return [
-            half_copy(slot, h, s_from, s_to, target),
-            remote(akv.at[s_from], akv.at[s_to], f_send.at[slot], f_recv.at[s_to - 1], target),
-            remote(bt.at[s_from], bt.at[s_to], t_send.at[slot], t_recv.at[s_to - 1], target),
+            remote(bkv.at[s_from, h], bkv.at[s_to, h], a_send.at[slot], a_recv.at[s_to - 1], to),
+            remote(akv.at[s_from], akv.at[s_to], f_send.at[slot], f_recv.at[s_to - 1], to),
+            remote(bt.at[s_from], bt.at[s_to], t_send.at[slot], t_recv.at[s_to - 1], to),
         ]
 
     def b_copies(slot, s_from, s_to, target):
-        return [half_copy(slot, other, s_from, s_to, target)]
-
-    near, far = at(e + 1, h), at(e + 2, h)
-    partner = at(e, other)
-
+        _, half, to = target
+        return [remote(bkv.at[s_from, half], bkv.at[s_to, half], b_send.at[slot], b_recv.at[s_to - 1], to)]
+
+    def ahead(by, turns):
+        half = jnp.where(turns, h, other)
+        return at(e + by, h), half, at(e + by, 1 - half)
+
+    near = ahead(1, jnp.logical_and(leaves, core == 1))
+    far = ahead(2, leaves)
     def start(copies):
         for copy in copies:
             copy.start()
@@ -120,17 +128,50 @@
             copy.wait_recv()
 
     def wait_b(s):
-        for copy in b_copies(0, s - 1, s, near):
+        for copy in b_copies(0, s - 1, s, (near[0], other, near[0])):
             copy.wait_recv()
 
-    ex_kv = remote(bkv.at[0, h], bkv.at[0, h], ex_send.at[0], ex_recv.at[0], partner)
-    ex_q = remote(bq.at[h], bq.at[h], ex_send.at[1], ex_recv.at[1], partner)
+    same, cross = at(across, h), at(across, other)
+    half_rows = HALF // 2
+
+    def q_part(half, i):
+        return bq.at[half, pl.ds(i * half_rows, half_rows)]
+
+    def out_copy(i, src, dst, target):
+        return remote(src, dst, ex_send.at[i], ex_recv.at[i], target)
+
+    kv_out = [
+        out_copy(0, bkv.at[0, h, 0], relay_kv.at[0], same),
+        out_copy(1, bkv.at[0, h, 1], relay_kv.at[1], cross),
+    ]
+    q_out = [
+        out_copy(2, q_part(h, 0), relay_q.at[0], same),
+        out_copy(3, q_part(h, 1), relay_q.at[1], cross),
+    ]
+    kv_on = [
+        out_copy(4, relay_kv.at[0], bkv.at[0, h, 0], cross),
+        out_copy(5, relay_kv.at[1], bkv.at[0, other, 1], same),
+    ]
+    q_on = [
+        out_copy(6, relay_q.at[0], q_part(h, 0), cross),
+        out_copy(7, relay_q.at[1], q_part(other, 1), same),
+    ]
+
+    def pass_on(arrived, onward):
+        for before, after in zip(arrived, onward):
+            before.wait_recv()
+            after.start()
+
+    def wait_all(copies):
+        for copy in copies:
+            copy.wait_recv()
+
     for copy in locals_[:4]:
         copy.wait()
-    ex_kv.start()
+    start(kv_out)
     first_sends(a_copies)
     locals_[4].wait()
-    ex_q.start()
+    start(q_out)
     locals_[5].wait()
 
     def scalars(s):
@@ -311,13 +352,15 @@
     prep_a(0)
     build_half(0, h)
     prep_aq()
+    pass_on(kv_out, kv_on)
     prep_q(h)
-    ex_kv.wait_recv()
-    first_sends(b_copies)
-    loop(lambda p: build_q(h, p), False)
     wait_a(1)
     forward_one(a_copies)
+    loop(lambda p: build_q(h, p), False)
+    wait_all(kv_on)
+    first_sends(b_copies)
     build_half(0, other)
+    pass_on(q_out, q_on)
     prep_a(1)
     build_half(1, h)
     wait_b(1)
@@ -327,7 +370,7 @@
     forward_two(a_copies)
     prep_a(2)
     build_half(2, h)
-    ex_q.wait_recv()
+    wait_all(q_on)
     prep_q(other)
     loop(lambda p: build_q(other, p), False)
     loop(own_position, True)
@@ -349,8 +392,8 @@
     write_log = pltpu.make_async_copy(log_ref, log_hbm, out_sem.at[2 * PAIRS])
     write_log.start()
 
-    ex_kv.wait_send()
-    ex_q.wait_send()
+    for copy in kv_out + q_out + kv_on + q_on:
+        copy.wait_send()
     for copies in (a_copies, b_copies):
         for copy in copies(0, 0, 1, near):
             copy.wait_send()
@@ -381,6 +424,8 @@
         in_specs=[pl.BlockSpec(memory_space=pltpu.SMEM)] + [hbm] * 6,
         out_specs=(hbm, hbm),
         scratch_shapes=[
+            pltpu.VMEM((2, HALF, 2 * DH), BF16),
+            pltpu.VMEM((2, HALF // 2, RQ * DH), BF16),
             pltpu.VMEM((heads, rows, DH), BF16),
             pltpu.VMEM((heads, rows), F32),
             pltpu.VMEM((4, 8, 128), jnp.int32),
@@ -405,8 +450,8 @@
             dma((heads + 1,)),
             dma((6,)),
             dma((4,)),
-            dma((2,)),
-            dma((2,)),
+            dma((8,)),
+            dma((8,)),
             dma((5,)),
             dma((3,)),
             dma((5,)),

time: 63.4 us -> 66.4 us (1.047)
  Pallas kernels: 58.7 us -> 62.3 us
    pallas_call x1, Pallas kernels: 58.7 us -> 62.3 us  [on_device(): pl.pallas_call(kernel, out_shape=(jax.ShapeDtypeStruct((heads, rows, DH),...]
where the time goes in v3:
time: 66.4 us; the launch traced here: 66.3 us
  Pallas kernels  62.3 us (94%)
  local copies, waits for them, and re-layouts  3.32 us (5%)
    pallas_call x1, Pallas kernels, on_device(): pl.pallas_call(kernel, out_shape=(jax.ShapeDtypeStruct((heads, rows, DH),...  62.3 us
    unnamed x4, local copies, waits for them, and re-layouts  3.32 us

profile of v3, /device:TPU:24, one launch (start us, length us, event | category | flops | bytes accessed | tf_op | source)
XLA Modules:
  0.0 66.3 jit_solution(10734502280804705362)
XLA Ops:
  0.6 62.3 %shard_map.86 = (bf16[16,384,128]{2,1,0:T(8,128)(2,1)}, f32[16,384]{1,0:T(8,128)}) custom-call(s32[1,2]{1,0:T(1,128)} %bt_in.1, bf16[6,16,384]{2,1,0:T(8,128)(2,1)} %aq_in.1, bf16[192,768]{1,0:T(8,128)(2,1)} %bq_in.1, bf16[2,16,384]{2,1,0:T(8,128)(2,1)} %ak_in.1, bf16[192,256]{1,0:T(8,128)(2,1)} %bk_in.1, bf16[2,16,384]{2,1,0:T(8,128)(2,1)} %av_in.1, ...), custom_call_target="tpu_custom_call" | custom-call | tf_op jit(solution)/shard_map/pallas_call | solution.py:418
  62.9 0.0 copy-start
  62.9 2.7 %copy.11 = bf16[16,384,128]{2,1,0:T(8,128)(2,1)} copy(bf16[16,384,128]{2,1,0:T(8,128)(2,1)} %get-tuple-element.4) | data formatting | bytes 3145728
  65.6 0.0 copy-done
  65.6 0.6 copy.12
Async XLA Ops:
  62.9 2.7 %copy-start = (f32[16,384]{1,0:T(8,128)S(1)}, f32[16,384]{1,0:T(8,128)}, u32[]{:S(2)}) copy-start(f32[16,384]{1,0:T(8,128)} %get-tuple-element.5) | copy-start | bytes 73732

commit v4 on v3

--- a/solution.py
+++ b/solution.py
@@ -23,7 +23,7 @@
     out_hbm, log_hbm,
     relay_kv, relay_q, out_ref, log_ref, bt, bts, aq, bq, bkv, akv,
     bqt, a2q, qbd, bkf, bvt, akt, avj, kb, vb,
-    o_acc, m_acc, l_acc, logs,
+    o_acc, m_acc, l_acc, logs, ident, spread,
     out_sem, local_sem, bts_sem, ex_send, ex_recv, a_send, a_recv, f_send, f_recv, t_send, t_recv, b_send, b_recv,
 ):
     e = lax.axis_index("blk")
@@ -75,6 +75,15 @@
     ]
     for copy in locals_:
         copy.start()
+    side = (2 * DH, 2 * DH)
+    ident[...] = (
+        lax.broadcasted_iota(jnp.int32, side, 0) == lax.broadcasted_iota(jnp.int32, side, 1)
+    ).astype(F32).astype(BF16)
+    side = (4 * PAIRS, 4 * DH)
+    source = lax.broadcasted_iota(jnp.int32, side, 0)
+    wanted = lax.broadcasted_iota(jnp.int32, side, 1) // DH * PAIRS
+    for p in range(PAIRS):
+        spread[p] = (source == wanted + p).astype(F32).astype(BF16)
     own0, own1 = bt_in[0, 0], bt_in[0, 1]
     tlane = lax.broadcasted_iota(jnp.int32, (8, 128), 1)
     bt[0] = jnp.where(tlane == 0, own0, own1)
@@ -108,15 +117,42 @@
         for copy in copies:
             copy.start()
 
-    def first_sends(copies):
-        start(copies(0, 0, 1, near))
-
-    def forward_one(copies):
+    last_core = jnp.logical_and(leaves, core == 1)
+    last_first = jnp.logical_and(leaves, core == 0)
+
+    def first_a():
+        start(a_copies(0, 0, 1, near))
+
+        @pl.when(last_core)
+        def _():
+            start(b_copies(0, 0, 1, near))
+
+    def first_b():
+        @pl.when(jnp.logical_not(last_core))
+        def _():
+            start(b_copies(0, 0, 1, near))
+
+    def forward_a():
         @pl.when(core == 0)
         def _():
-            start(copies(1, 1, 2, near))
-            start(copies(2, 0, 2, far))
-            start(copies(3, 1, 3, far))
+            start(a_copies(1, 1, 2, near))
+            start(a_copies(2, 0, 2, far))
+            start(a_copies(3, 1, 3, far))
+
+        @pl.when(last_first)
+        def _():
+            start(b_copies(2, 0, 2, far))
+            start(b_copies(3, 1, 3, far))
+
+    def forward_b():
+        @pl.when(core == 0)
+        def _():
+            start(b_copies(1, 1, 2, near))
+
+        @pl.when(jnp.logical_and(core == 0, jnp.logical_not(leaves)))
+        def _():
+            start(b_copies(2, 0, 2, far))
+            start(b_copies(3, 1, 3, far))
 
     def forward_two(copies):
         @pl.when(core == 0)
@@ -169,7 +205,7 @@
     for copy in locals_[:4]:
         copy.wait()
     start(kv_out)
-    first_sends(a_copies)
+    first_a()
     locals_[4].wait()
     start(q_out)
     locals_[5].wait()
@@ -181,24 +217,30 @@
         b0, b1 = bts[s, 0, 0], bts[s, 0, 1]
         return (b0 > b1).astype(jnp.int32), jnp.minimum(b0, b1)
 
+    def dot(x, y):
+        return jnp.dot(x, y, preferred_element_type=F32)
+
+    def turn(y):
+        n = y.shape[1]
+        return lax.dot_general(ident[:n, :n], y, (((1,), (1,)), ((), ())), preferred_element_type=F32)
+
     def prep_a(s):
-        x = akv[s].astype(F32)
-        keys = x[0:2].reshape(32, 2 * HALF)
-        keys_t = jnp.concatenate([keys, jnp.zeros((96, 2 * HALF), F32)], axis=0).T
-        akt[s, 0] = keys_t[:HALF]
-        akt[s, 1] = keys_t[HALF:]
-        avj[s, 0] = x[2:4, :, :HALF]
-        avj[s, 1] = x[2:4, :, HALF:]
+        keys = akv[s, 0:2].reshape(4 * PAIRS, 2 * HALF)
+        keys_t = jnp.concatenate([turn(keys[:, i * DH : (i + 1) * DH]) for i in range(3)], axis=0)
+        akt[s, 0] = keys_t[:HALF].astype(BF16)
+        akt[s, 1] = keys_t[HALF:].astype(BF16)
+        values = akv[s, 2:4].astype(F32)
+        avj[s, 0] = values[:, :, :HALF]
+        avj[s, 1] = values[:, :, HALF:]
 
     def prep_b(s, j):
         bkf[s, j] = bkv[s, j, 0].astype(F32)
-        v = bkv[s, j, 1].astype(F32)
-        v = jnp.concatenate([v, jnp.zeros((64, 2 * DH), F32)], axis=0).T
-        bvt[s, j] = v[:, :HALF]
+        bvt[s, j] = turn(bkv[s, j, 1])
 
     def prep_q(j):
-        b = bq[j].astype(F32)
-        bqt[j] = jnp.concatenate([b, b], axis=0).T.astype(BF16)
+        for i in range(RQ // 2):
+            b = bq[j, :, i * 2 * DH : (i + 1) * 2 * DH]
+            bqt[j, i * 2 * DH : (i + 1) * 2 * DH] = turn(jnp.concatenate([b, b], axis=0))
 
     def prep_aq():
         x = aq[...].astype(F32)
@@ -212,18 +254,18 @@
         a2q[1] = jnp.where(wide, turned(low), high)
 
     def build_q(j, p):
-        total = a2q[j, 0, pl.ds(p, 1), :] * bqt[j, 0:DH, :].astype(F32)
+        total = a2q[j, 0, pl.ds(p, 1), :] * bqt[j, 0:DH, :]
         for r in range(1, RQ):
-            total += a2q[j, r, pl.ds(p, 1), :] * bqt[j, r * DH : (r + 1) * DH, :].astype(F32)
+            total += a2q[j, r, pl.ds(p, 1), :] * bqt[j, r * DH : (r + 1) * DH, :]
         total = total * (1.0 / RQ)
         qbd[j, p, 0:DH] = jnp.where(first, total, 0.0).astype(BF16)
         qbd[j, p, DH : 2 * DH] = jnp.where(first, 0.0, total).astype(BF16)
 
     def build_kv(s, j, p):
-        a = pltpu.roll(akt[s, j], lax.rem(128 - p, 128), 1)
+        wide = dot(akt[s, j], spread[p])
         b0, b1 = bkf[s, j, :, 0:DH], bkf[s, j, :, DH : 2 * DH]
-        ka = a[:, 0:1] * b0 + a[:, 16:17] * b1
-        kb_ = a[:, 8:9] * b0 + a[:, 24:25] * b1
+        ka = wide[:, 0:DH] * b0 + wide[:, 2 * DH : 3 * DH] * b1
+        kb_ = wide[:, DH : 2 * DH] * b0 + wide[:, 3 * DH :] * b1
         c0, c1 = bvt[s, j, 0:DH], bvt[s, j, DH : 2 * DH]
         va = avj[s, j, 0, pl.ds(p, 1), :] * c0 + avj[s, j, 1, pl.ds(p, 1), :] * c1
         vb_ = avj[s, j, 0, pl.ds(p + PAIRS, 1), :] * c0 + avj[s, j, 1, pl.ds(p + PAIRS, 1), :] * c1
@@ -231,9 +273,6 @@
         kb[s, j, p, :, DH : 2 * DH] = kb_.astype(BF16)
         vb[s, j, p, 0:DH] = va.astype(BF16)
         vb[s, j, p, DH : 2 * DH] = vb_.astype(BF16)
-
-    def dot(x, y):
-        return jnp.dot(x, y, preferred_element_type=F32)
 
     middle = lax.broadcasted_iota(jnp.int32, (1, DH), 1) < HALF - DH
 
@@ -251,22 +290,21 @@
     def highest(scores):
         return jnp.max(scores, axis=0, keepdims=True)
 
-    def loop(body, both):
+    def loop(body, width):
+        each = PAIRS // width
+
         def step(p, carry):
-            if both:
-                done = [body(p), body(p + PAIRS // 2)]
-            else:
-                done = [body(p)]
+            done = [body(p + i * each) for i in range(width)]
             for store in done:
                 if store is not None:
                     store()
             return carry
 
-        lax.fori_loop(0, PAIRS // 2 if both else PAIRS, step, 0)
+        lax.fori_loop(0, each, step, 0)
 
     def build_half(s, j):
         prep_b(s, j)
-        loop(lambda p: build_kv(s, j, p), False)
+        loop(lambda p: build_kv(s, j, p), 4)
 
     def put(which, p, state):
         m_acc[which, p], l_acc[which, p], o_acc[which, p] = state
@@ -328,8 +366,8 @@
                     put(0, p, (low, l_low, o_low))
                     put(1, p, (high, l_high, o_high))
                     return
-                rows_low = (o_low * (0.5 / l_low)).T.astype(BF16)
-                rows_high = (o_high * (0.5 / l_high)).T.astype(BF16)
+                rows_low = turned_rows((o_low * (0.5 / l_low)).astype(BF16))
+                rows_high = turned_rows((o_high * (0.5 / l_high)).astype(BF16))
                 log_low = low * SCALE + jnp.log(l_low)
                 log_high = high * SCALE + jnp.log(l_high)
                 for j in range(2):
@@ -343,28 +381,32 @@
 
             return store
 
-        loop(body, True)
+        loop(body, 2)
+
+    def turned_rows(x):
+        parts = [turn(x[:, i * DH : (i + 1) * DH]) for i in range(3)]
+        return jnp.concatenate(parts, axis=0).astype(BF16)
 
     def write_out(head):
         return pltpu.make_async_copy(out_ref.at[head], out_hbm.at[head], out_sem.at[head])
 
     jl0, low0 = scalars(0)
     prep_a(0)
+    prep_aq()
     build_half(0, h)
-    prep_aq()
     pass_on(kv_out, kv_on)
     prep_q(h)
+    loop(lambda p: build_q(h, p), 1)
     wait_a(1)
-    forward_one(a_copies)
-    loop(lambda p: build_q(h, p), False)
+    forward_a()
+    pass_on(q_out, q_on)
     wait_all(kv_on)
-    first_sends(b_copies)
+    first_b()
     build_half(0, other)
-    pass_on(q_out, q_on)
     prep_a(1)
     build_half(1, h)
     wait_b(1)
-    forward_one(b_copies)
+    forward_b()
     build_half(1, other)
     wait_a(2)
     forward_two(a_copies)
@@ -372,8 +414,8 @@
     build_half(2, h)
     wait_all(q_on)
     prep_q(other)
-    loop(lambda p: build_q(other, p), False)
-    loop(own_position, True)
+    loop(lambda p: build_q(other, p), 1)
+    loop(own_position, 2)
     wait_b(2)
     forward_two(b_copies)
     earlier_position(1)
@@ -434,12 +476,12 @@
             pltpu.VMEM((2, HALF, RQ * DH), BF16),
             pltpu.VMEM((4, 2, 2, HALF, 2 * DH), BF16),
             pltpu.VMEM((4, 4, heads, rows), BF16),
-            pltpu.VMEM((2, RQ * DH, rows), BF16),
+            pltpu.VMEM((2, RQ * DH, rows), F32),
             pltpu.VMEM((2, RQ, PAIRS, rows), F32),
             pltpu.VMEM((2, PAIRS, 2 * DH, rows), BF16),
             pltpu.VMEM((4, 2, HALF, 2 * DH), F32),
             pltpu.VMEM((4, 2, 2 * DH, HALF), F32),
-            pltpu.VMEM((4, 2, HALF, 128), F32),
+            pltpu.VMEM((4, 2, HALF, 4 * PAIRS), BF16),
             pltpu.VMEM((4, 2, 2, heads, HALF), F32),
             pltpu.VMEM((4, 2, PAIRS, HALF, 2 * DH), BF16),
             pltpu.VMEM((4, 2, PAIRS, 2 * DH, HALF), BF16),
@@ -447,6 +489,8 @@
             pltpu.VMEM((2, PAIRS, 1, rows), F32),
             pltpu.VMEM((2, PAIRS, 1, rows), F32),
             pltpu.VMEM((2, PAIRS, rows), F32),
+            pltpu.VMEM((2 * DH, 2 * DH), BF16),
+            pltpu.VMEM((PAIRS, 4 * PAIRS, 4 * DH), BF16),
             dma((heads + 1,)),
             dma((6,)),
             dma((4,)),

time: 66.4 us -> 57.1 us (0.86)
  the two profiles are of different devices: /device:TPU:24 before, /device:TPU:16 now
where the time goes in v4:
time: 57.1 us; the launch traced here: 56.9 us
  Pallas kernels  52.9 us (93%)
  local copies, waits for them, and re-layouts  3.32 us (6%)
  between operations  0.65 us (1%)
    pallas_call x1, Pallas kernels, on_device(): pl.pallas_call(kernel, out_shape=(jax.ShapeDtypeStruct((heads, rows, DH),...  52.9 us
    unnamed x4, local copies, waits for them, and re-layouts  3.32 us

profile of v4, /device:TPU:16, one launch (start us, length us, event | category | flops | bytes accessed | tf_op | source)
XLA Modules:
  0.0 56.9 jit_solution(973002689883764724)
XLA Ops:
  0.6 52.9 %shard_map.86 = (bf16[16,384,128]{2,1,0:T(8,128)(2,1)}, f32[16,384]{1,0:T(8,128)}) custom-call(s32[1,2]{1,0:T(1,128)} %bt_in.1, bf16[6,16,384]{2,1,0:T(8,128)(2,1)} %aq_in.1, bf16[192,768]{1,0:T(8,128)(2,1)} %bq_in.1, bf16[2,16,384]{2,1,0:T(8,128)(2,1)} %ak_in.1, bf16[192,256]{1,0:T(8,128)(2,1)} %bk_in.1, bf16[2,16,384]{2,1,0:T(8,128)(2,1)} %av_in.1, ...), custom_call_target="tpu_custom_call" | custom-call | tf_op jit(solution)/shard_map/pallas_call | solution.py:460
  53.6 0.0 copy-start
  53.6 2.7 %copy.11 = bf16[16,384,128]{2,1,0:T(8,128)(2,1)} copy(bf16[16,384,128]{2,1,0:T(8,128)(2,1)} %get-tuple-element.4) | data formatting | bytes 3145728
  56.3 0.0 copy-done
  56.3 0.6 %copy.12 = f32[16,384]{1,0:T(8,128)} copy(f32[16,384]{1,0:T(8,128)S(1)} %copy-done) | data formatting | bytes 49152
Async XLA Ops:
  53.6 2.7 %copy-start = (f32[16,384]{1,0:T(8,128)S(1)}, f32[16,384]{1,0:T(8,128)}, u32[]{:S(2)}) copy-start(f32[16,384]{1,0:T(8,128)} %get-tuple-element.5) | copy-start | bytes 73732

commit v5 on v4

--- a/solution.py
+++ b/solution.py
@@ -39,7 +39,7 @@
 
     across = e + places // 2
     chip = lax.rem(e // 2, places // 4)
-    leaves = chip == places // 4 - 1
+    leaves = jnp.logical_and(chip == places // 4 - 1, core == 1)
     enters = jnp.logical_and(chip == 0, core == 0)
 
     barrier = pltpu.get_barrier_semaphore()
@@ -51,14 +51,9 @@
     greet(at(across, other))
     greet(at(e - 1, h))
 
-    @pl.when(core == 0)
-    def _():
-        greet(at(e - 2, h))
-
     @pl.when(enters)
     def _():
         greet(at(e - 1, other))
-        greet(at(e - 2, other))
 
     locals_ = [
         pltpu.make_async_copy(src, dst, local_sem.at[i])
@@ -87,85 +82,61 @@
     own0, own1 = bt_in[0, 0], bt_in[0, 1]
     tlane = lax.broadcasted_iota(jnp.int32, (8, 128), 1)
     bt[0] = jnp.where(tlane == 0, own0, own1)
-
-    pl.semaphore_wait(barrier, 4 - core + leaves.astype(jnp.int32))
+    pltpu.make_async_copy(bt.at[0], bts.at[0], bts_sem.at[0]).start()
+
+    pl.semaphore_wait(barrier, 3 + leaves.astype(jnp.int32))
 
     def remote(src, dst, send, recv, target):
         return pltpu.make_async_remote_copy(
             src_ref=src, dst_ref=dst, send_sem=send, recv_sem=recv, device_id=target, device_id_type=MESH
         )
 
-    def a_copies(slot, s_from, s_to, target):
-        to = target[0]
+    ahead = at(e + 1, h)
+    half = jnp.where(leaves, h, other)
+    ahead_b = at(e + 1, 1 - half)
+
+    def a_copies(s):
         return [
-            remote(bkv.at[s_from, h], bkv.at[s_to, h], a_send.at[slot], a_recv.at[s_to - 1], to),
-            remote(akv.at[s_from], akv.at[s_to], f_send.at[slot], f_recv.at[s_to - 1], to),
-            remote(bt.at[s_from], bt.at[s_to], t_send.at[slot], t_recv.at[s_to - 1], to),
+            remote(bkv.at[s, h], bkv.at[s + 1, h], a_send.at[s], a_recv.at[s], ahead),
+            remote(akv.at[s], akv.at[s + 1], f_send.at[s], f_recv.at[s], ahead),
+            remote(bt.at[s], bt.at[s + 1], t_send.at[s], t_recv.at[s], ahead),
         ]
 
-    def b_copies(slot, s_from, s_to, target):
-        _, half, to = target
-        return [remote(bkv.at[s_from, half], bkv.at[s_to, half], b_send.at[slot], b_recv.at[s_to - 1], to)]
-
-    def ahead(by, turns):
-        half = jnp.where(turns, h, other)
-        return at(e + by, h), half, at(e + by, 1 - half)
-
-    near = ahead(1, jnp.logical_and(leaves, core == 1))
-    far = ahead(2, leaves)
+    def b_copy(s):
+        return remote(bkv.at[s, half], bkv.at[s + 1, half], b_send.at[s], b_recv.at[s], ahead_b)
+
     def start(copies):
         for copy in copies:
             copy.start()
 
-    last_core = jnp.logical_and(leaves, core == 1)
-    last_first = jnp.logical_and(leaves, core == 0)
-
-    def first_a():
-        start(a_copies(0, 0, 1, near))
-
-        @pl.when(last_core)
+    def send_a(s):
+        start(a_copies(s))
+
+        @pl.when(leaves)
         def _():
-            start(b_copies(0, 0, 1, near))
-
-    def first_b():
-        @pl.when(jnp.logical_not(last_core))
+            b_copy(s).start()
+
+    def send_b(s):
+        @pl.when(jnp.logical_not(leaves))
         def _():
-            start(b_copies(0, 0, 1, near))
-
-    def forward_a():
-        @pl.when(core == 0)
-        def _():
-            start(a_copies(1, 1, 2, near))
-            start(a_copies(2, 0, 2, far))
-            start(a_copies(3, 1, 3, far))
-
-        @pl.when(last_first)
-        def _():
-            start(b_copies(2, 0, 2, far))
-            start(b_copies(3, 1, 3, far))
-
-    def forward_b():
-        @pl.when(core == 0)
-        def _():
-            start(b_copies(1, 1, 2, near))
-
-        @pl.when(jnp.logical_and(core == 0, jnp.logical_not(leaves)))
-        def _():
-            start(b_copies(2, 0, 2, far))
-            start(b_copies(3, 1, 3, far))
-
-    def forward_two(copies):
-        @pl.when(core == 0)
-        def _():
-            start(copies(4, 2, 3, near))
+            b_copy(s).start()
+
+    def fetch(s):
+        return pltpu.make_async_copy(bt.at[s], bts.at[s], bts_sem.at[s])
 
     def wait_a(s):
-        for copy in a_copies(0, s - 1, s, near):
+        for copy in a_copies(s - 1):
             copy.wait_recv()
+        fetch(s).start()
+        if s < 3:
+            send_a(s)
 
     def wait_b(s):
-        for copy in b_copies(0, s - 1, s, (near[0], other, near[0])):
-            copy.wait_recv()
+        remote(
+            bkv.at[s - 1, other], bkv.at[s, other], b_send.at[s - 1], b_recv.at[s - 1], ahead
+        ).wait_recv()
+        if s < 3:
+            send_b(s)
 
     same, cross = at(across, h), at(across, other)
     half_rows = HALF // 2
@@ -205,15 +176,13 @@
     for copy in locals_[:4]:
         copy.wait()
     start(kv_out)
-    first_a()
+    send_a(0)
     locals_[4].wait()
     start(q_out)
     locals_[5].wait()
 
     def scalars(s):
-        copy = pltpu.make_async_copy(bt.at[s], bts.at[s], bts_sem.at[s])
-        copy.start()
-        copy.wait()
+        fetch(s).wait()
         b0, b1 = bts[s, 0, 0], bts[s, 0, 1]
         return (b0 > b1).astype(jnp.int32), jnp.minimum(b0, b1)
 
@@ -312,54 +281,65 @@
     def get(which, p):
         return m_acc[which, p], l_acc[which, p], o_acc[which, p]
 
-    def own_position(p):
-        k_low, v_low = kb[0, jl0, p], vb[0, jl0, p]
-        k_high, v_high = kb[0, 1 - jl0, p], vb[0, 1 - jl0, p]
-        q_low, q_high = qbd[jl0, p], qbd[1 - jl0, p]
+    def scores_of(s, j_keys, j_queries, p):
+        return dot(kb[s, j_keys, p], qbd[j_queries, p])
+
+    def own_blocks(p):
         shape = (HALF, 2 * HALF)
         row = lax.broadcasted_iota(jnp.int32, shape, 0)
         col = lax.broadcasted_iota(jnp.int32, shape, 1)
         seen = row <= jnp.where(col < HALF, col, col - HALF)
-        low = jnp.where(seen, dot(k_low, q_low), MASKED)
-        cross = dot(k_low, q_high)
-        high = jnp.where(seen, dot(k_high, q_high), MASKED)
-        m_low = highest(low)
-        m_high = jnp.maximum(highest(cross), highest(high))
-        l_low, o_low = weigh(low, m_low, v_low)
-        l_cross, o_cross = weigh(cross, m_high, v_low)
-        l_high, o_high = weigh(high, m_high, v_high)
-
-        def store():
-            put(0, p, (m_low, l_low, o_low))
-            put(1, p, (m_high, l_cross + l_high, o_cross + o_high))
-
-        return store
-
-    def earlier_position(s, last=False):
+        low = jnp.where(seen, scores_of(0, jl0, jl0, p), MASKED)
+        cross = scores_of(0, jl0, 1 - jl0, p)
+        high = jnp.where(seen, scores_of(0, 1 - jl0, 1 - jl0, p), MASKED)
+        v_low, v_high = vb[0, jl0, p], vb[0, 1 - jl0, p]
+        return [(low, v_low)], [(cross, v_low), (high, v_high)]
+
+    def choose(s):
         jls, lows = scalars(s)
         pick = (lows > low0).astype(jnp.int32)
-        jq = jl0 + pick - 2 * jl0 * pick
-        jk = jls + pick - 2 * jls * pick
-        is_high = pick == 1
+        return s, jls, jls + pick - 2 * jls * pick, jl0 + pick - 2 * jl0 * pick, pick == 1
+
+    def attend(offsets, last):
+        chosen = [choose(s) for s in offsets]
 
         def body(p):
-            m_low, l_low, o_low = get(0, p)
-            m_high, l_high, o_high = get(1, p)
-            k1, v1, q1 = kb[s, jls, p], vb[s, jls, p], qbd[1 - jl0, p]
-            k2, v2, q2 = kb[s, jk, p], vb[s, jk, p], qbd[jq, p]
-            s1 = dot(k1, q1)
-            s2 = dot(k2, q2)
-            top1, top2 = highest(s1), highest(s2)
-            high = jnp.maximum(jnp.maximum(m_high, top1), jnp.where(is_high, top2, MASKED))
-            low = jnp.maximum(m_low, jnp.where(is_high, MASKED, top2))
-            t1, o1 = weigh(s1, high, v1)
-            t2, o2 = weigh(s2, jnp.where(is_high, high, low), v2)
-            r_high = jnp.exp((m_high - high) * SCALE)
-            r_low = jnp.exp((m_low - low) * SCALE)
-            l_high = l_high * r_high + t1 + jnp.where(is_high, t2, 0.0)
-            l_low = l_low * r_low + jnp.where(is_high, 0.0, t2)
-            o_high = o_high * r_high + o1 + jnp.where(is_high, o2, 0.0)
-            o_low = o_low * r_low + jnp.where(is_high, 0.0, o2)
+            if last:
+                low_blocks, high_blocks = [], []
+                m_low, l_low, o_low = get(0, p)
+                m_high, l_high, o_high = get(1, p)
+                low_tops, high_tops = [m_low], [m_high]
+            else:
+                low_blocks, high_blocks = own_blocks(p)
+                low_tops, high_tops = [], []
+            floating = []
+            for s, jls, jk, jq, is_high in chosen:
+                high_blocks.append((scores_of(s, jls, 1 - jl0, p), vb[s, jls, p]))
+                scores = scores_of(s, jk, jq, p)
+                floating.append((scores, vb[s, jk, p], is_high))
+                top = highest(scores)
+                high_tops.append(jnp.where(is_high, top, MASKED))
+                low_tops.append(jnp.where(is_high, MASKED, top))
+            low_tops += [highest(scores) for scores, _ in low_blocks]
+            high_tops += [highest(scores) for scores, _ in high_blocks]
+            low, high = low_tops[0], high_tops[0]
+            for top in low_tops[1:]:
+                low = jnp.maximum(low, top)
+            for top in high_tops[1:]:
+                high = jnp.maximum(high, top)
+            low_parts = [weigh(scores, low, values) for scores, values in low_blocks]
+            high_parts = [weigh(scores, high, values) for scores, values in high_blocks]
+            for scores, values, is_high in floating:
+                total, out = weigh(scores, jnp.where(is_high, high, low), values)
+                high_parts.append((jnp.where(is_high, total, 0.0), jnp.where(is_high, out, 0.0)))
+                low_parts.append((jnp.where(is_high, 0.0, total), jnp.where(is_high, 0.0, out)))
+            if last:
+                fade = jnp.exp((m_low - low) * SCALE)
+                low_parts.append((l_low * fade, o_low * fade))
+                fade = jnp.exp((m_high - high) * SCALE)
+                high_parts.append((l_high * fade, o_high * fade))
+            l_low, o_low = (sum(parts[1:], parts[0]) for parts in zip(*low_parts))
+            l_high, o_high = (sum(parts[1:], parts[0]) for parts in zip(*high_parts))
 
             def store():
                 if not last:
@@ -394,39 +374,33 @@
     prep_a(0)
     prep_aq()
     build_half(0, h)
+    wait_a(1)
     pass_on(kv_out, kv_on)
     prep_q(h)
     loop(lambda p: build_q(h, p), 1)
-    wait_a(1)
-    forward_a()
     pass_on(q_out, q_on)
-    wait_all(kv_on)
-    first_b()
-    build_half(0, other)
     prep_a(1)
     build_half(1, h)
+    wait_a(2)
+    wait_all(kv_on)
+    send_b(0)
+    build_half(0, other)
     wait_b(1)
-    forward_b()
-    build_half(1, other)
-    wait_a(2)
-    forward_two(a_copies)
     prep_a(2)
     build_half(2, h)
+    build_half(1, other)
+    wait_b(2)
     wait_all(q_on)
     prep_q(other)
     loop(lambda p: build_q(other, p), 1)
-    loop(own_position, 2)
-    wait_b(2)
-    forward_two(b_copies)
-    earlier_position(1)
     build_half(2, other)
-    earlier_position(2)
+    attend([1], False)
     wait_a(3)
     prep_a(3)
     build_half(3, h)
     wait_b(3)
     build_half(3, other)
-    earlier_position(3, last=True)
+    attend([2, 3], True)
     log0, log1 = logs[0], logs[1]
     log_ref[0:PAIRS] = jnp.where(first, log0, pltpu.roll(log1, HALF, 1))
     log_ref[PAIRS:] = jnp.where(first, pltpu.roll(log0, HALF, 1), log1)
@@ -436,16 +410,9 @@
 
     for copy in kv_out + q_out + kv_on + q_on:
         copy.wait_send()
-    for copies in (a_copies, b_copies):
-        for copy in copies(0, 0, 1, near):
+    for s in range(3):
+        for copy in a_copies(s) + [b_copy(s)]:
             copy.wait_send()
-
-    @pl.when(core == 0)
-    def _():
-        for copies in (a_copies, b_copies):
-            for slot in range(1, 5):
-                for copy in copies(slot, 0, 1, near):
-                    copy.wait_send()
 
     for head in range(2 * PAIRS):
         write_out(head).wait()
@@ -496,13 +463,13 @@
             dma((4,)),
             dma((8,)),
             dma((8,)),
-            dma((5,)),
-            dma((3,)),
-            dma((5,)),
-            dma((3,)),
-            dma((5,)),
-            dma((3,)),
-            dma((5,)),
+            dma((3,)),
+            dma((3,)),
+            dma((3,)),
+            dma((3,)),
+            dma((3,)),
+            dma((3,)),
+            dma((3,)),
             dma((3,)),
         ],
         compiler_params=pltpu.CompilerParams(

time: 57.1 us -> 54.6 us (0.956)
  the two profiles are of different devices: /device:TPU:16 before, /device:TPU:2 now
where the time goes in v5:
time: 54.6 us; the launch traced here: 54.4 us
  Pallas kernels  50.5 us (92%)
  local copies, waits for them, and re-layouts  3.32 us (6%)
  between operations  0.65 us (1%)
    pallas_call x1, Pallas kernels, on_device(): pl.pallas_call(kernel, out_shape=(jax.ShapeDtypeStruct((heads, rows, DH),...  50.5 us
    unnamed x4, local copies, waits for them, and re-layouts  3.32 us

profile of v5, /device:TPU:2, one launch (start us, length us, event | category | flops | bytes accessed | tf_op | source)
XLA Modules:
  0.0 54.4 jit_solution(17643094467076078473)
XLA Ops:
  0.6 50.5 %shard_map.86 = (bf16[16,384,128]{2,1,0:T(8,128)(2,1)}, f32[16,384]{1,0:T(8,128)}) custom-call(s32[1,2]{1,0:T(1,128)} %bt_in.1, bf16[6,16,384]{2,1,0:T(8,128)(2,1)} %aq_in.1, bf16[192,768]{1,0:T(8,128)(2,1)} %bq_in.1, bf16[2,16,384]{2,1,0:T(8,128)(2,1)} %ak_in.1, bf16[192,256]{1,0:T(8,128)(2,1)} %bk_in.1, bf16[2,16,384]{2,1,0:T(8,128)(2,1)} %av_in.1, ...), custom_call_target="tpu_custom_call" | custom-call | tf_op jit(solution)/shard_map/pallas_call | solution.py:427
  51.1 0.0 copy-start
  51.1 2.7 %copy.11 = bf16[16,384,128]{2,1,0:T(8,128)(2,1)} copy(bf16[16,384,128]{2,1,0:T(8,128)(2,1)} %get-tuple-element.4) | data formatting | bytes 3145728
  53.8 0.0 copy-done
  53.8 0.6 %copy.12 = f32[16,384]{1,0:T(8,128)} copy(f32[16,384]{1,0:T(8,128)S(1)} %copy-done) | data formatting | bytes 49152
Async XLA Ops:
  51.1 2.7 %copy-start = (f32[16,384]{1,0:T(8,128)S(1)}, f32[16,384]{1,0:T(8,128)}, u32[]{:S(2)}) copy-start(f32[16,384]{1,0:T(8,128)} %get-tuple-element.5) | copy-start | bytes 73732

commit v6 on v5

--- a/solution.py
+++ b/solution.py
@@ -300,11 +300,11 @@
         pick = (lows > low0).astype(jnp.int32)
         return s, jls, jls + pick - 2 * jls * pick, jl0 + pick - 2 * jl0 * pick, pick == 1
 
-    def attend(offsets, last):
+    def attend(offsets, width, last=False):
         chosen = [choose(s) for s in offsets]
 
         def body(p):
-            if last:
+            if offsets:
                 low_blocks, high_blocks = [], []
                 m_low, l_low, o_low = get(0, p)
                 m_high, l_high, o_high = get(1, p)
@@ -333,7 +333,7 @@
                 total, out = weigh(scores, jnp.where(is_high, high, low), values)
                 high_parts.append((jnp.where(is_high, total, 0.0), jnp.where(is_high, out, 0.0)))
                 low_parts.append((jnp.where(is_high, 0.0, total), jnp.where(is_high, 0.0, out)))
-            if last:
+            if offsets:
                 fade = jnp.exp((m_low - low) * SCALE)
                 low_parts.append((l_low * fade, o_low * fade))
                 fade = jnp.exp((m_high - high) * SCALE)
@@ -361,7 +361,7 @@
 
             return store
 
-        loop(body, 2)
+        loop(body, width)
 
     def turned_rows(x):
         parts = [turn(x[:, i * DH : (i + 1) * DH]) for i in range(3)]
@@ -374,33 +374,34 @@
     prep_a(0)
     prep_aq()
     build_half(0, h)
-    wait_a(1)
     pass_on(kv_out, kv_on)
     prep_q(h)
     loop(lambda p: build_q(h, p), 1)
     pass_on(q_out, q_on)
-    prep_a(1)
-    build_half(1, h)
-    wait_a(2)
     wait_all(kv_on)
     send_b(0)
     build_half(0, other)
-    wait_b(1)
-    prep_a(2)
-    build_half(2, h)
-    build_half(1, other)
-    wait_b(2)
+    wait_a(1)
     wait_all(q_on)
     prep_q(other)
     loop(lambda p: build_q(other, p), 1)
+    prep_a(1)
+    build_half(1, h)
+    attend([], 2)
+    wait_a(2)
+    wait_b(1)
+    build_half(1, other)
+    prep_a(2)
+    build_half(2, h)
+    wait_b(2)
+    attend([1], 4)
     build_half(2, other)
-    attend([1], False)
     wait_a(3)
     prep_a(3)
     build_half(3, h)
     wait_b(3)
     build_half(3, other)
-    attend([2, 3], True)
+    attend([2, 3], 2, last=True)
     log0, log1 = logs[0], logs[1]
     log_ref[0:PAIRS] = jnp.where(first, log0, pltpu.roll(log1, HALF, 1))
     log_ref[PAIRS:] = jnp.where(first, pltpu.roll(log0, HALF, 1), log1)

time: 54.6 us -> 53.5 us (0.980)
  the two profiles are of different devices: /device:TPU:2 before, /device:TPU:24 now
where the time goes in v6:
time: 53.5 us; the launch traced here: 53.4 us
  Pallas kernels  49.4 us (92%)
  local copies, waits for them, and re-layouts  3.32 us (6%)
  between operations  0.65 us (1%)
    pallas_call x1, Pallas kernels, on_device(): pl.pallas_call(kernel, out_shape=(jax.ShapeDtypeStruct((heads, rows, DH),...  49.4 us
    unnamed x4, local copies, waits for them, and re-layouts  3.32 us

profile of v6, /device:TPU:24, one launch (start us, length us, event | category | flops | bytes accessed | tf_op | source)
XLA Modules:
  0.0 53.4 jit_solution(10854683871031448702)
XLA Ops:
  0.6 49.4 %shard_map.86 = (bf16[16,384,128]{2,1,0:T(8,128)(2,1)}, f32[16,384]{1,0:T(8,128)}) custom-call(s32[1,2]{1,0:T(1,128)} %bt_in.1, bf16[6,16,384]{2,1,0:T(8,128)(2,1)} %aq_in.1, bf16[192,768]{1,0:T(8,128)(2,1)} %bq_in.1, bf16[2,16,384]{2,1,0:T(8,128)(2,1)} %ak_in.1, bf16[192,256]{1,0:T(8,128)(2,1)} %bk_in.1, bf16[2,16,384]{2,1,0:T(8,128)(2,1)} %av_in.1, ...), custom_call_target="tpu_custom_call" | custom-call | tf_op jit(solution)/shard_map/pallas_call | solution.py:428
  50.0 0.0 copy-start
  50.0 2.7 %copy.11 = bf16[16,384,128]{2,1,0:T(8,128)(2,1)} copy(bf16[16,384,128]{2,1,0:T(8,128)(2,1)} %get-tuple-element.4) | data formatting | bytes 3145728
  52.7 0.0 copy-done
  52.7 0.6 %copy.12 = f32[16,384]{1,0:T(8,128)} copy(f32[16,384]{1,0:T(8,128)S(1)} %copy-done) | data formatting | bytes 49152
Async XLA Ops:
  50.0 2.7 %copy-start = (f32[16,384]{1,0:T(8,128)S(1)}, f32[16,384]{1,0:T(8,128)}, u32[]{:S(2)}) copy-start(f32[16,384]{1,0:T(8,128)} %get-tuple-element.5) | copy-start | bytes 73732

commit v7 on v6

--- a/solution.py
+++ b/solution.py
@@ -22,10 +22,11 @@
     bt_in, aq_in, bq_in, ak_in, bk_in, av_in, bv_in,
     out_hbm, log_hbm,
     relay_kv, relay_q, out_ref, log_ref, bt, bts, aq, bq, bkv, akv,
-    bqt, a2q, qbd, bkf, bvt, akt, avj, kb, vb,
+    bqt, a2q, qbd, bkf, bvt, akt, avj, kb0, kb1, kb2, kb3, vb0, vb1, vb2, vb3,
     o_acc, m_acc, l_acc, logs, ident, spread,
     out_sem, local_sem, bts_sem, ex_send, ex_recv, a_send, a_recv, f_send, f_recv, t_send, t_recv, b_send, b_recv,
 ):
+    kb, vb = (kb0, kb1, kb2, kb3), (vb0, vb1, vb2, vb3)
     e = lax.axis_index("blk")
     h = lax.axis_index("head")
     places = lax.axis_size("blk")
@@ -238,10 +239,10 @@
         c0, c1 = bvt[s, j, 0:DH], bvt[s, j, DH : 2 * DH]
         va = avj[s, j, 0, pl.ds(p, 1), :] * c0 + avj[s, j, 1, pl.ds(p, 1), :] * c1
         vb_ = avj[s, j, 0, pl.ds(p + PAIRS, 1), :] * c0 + avj[s, j, 1, pl.ds(p + PAIRS, 1), :] * c1
-        kb[s, j, p, :, 0:DH] = ka.astype(BF16)
-        kb[s, j, p, :, DH : 2 * DH] = kb_.astype(BF16)
-        vb[s, j, p, 0:DH] = va.astype(BF16)
-        vb[s, j, p, DH : 2 * DH] = vb_.astype(BF16)
+        kb[s][j, p, :, 0:DH] = ka.astype(BF16)
+        kb[s][j, p, :, DH : 2 * DH] = kb_.astype(BF16)
+        vb[s][j, p, 0:DH] = va.astype(BF16)
+        vb[s][j, p, DH : 2 * DH] = vb_.astype(BF16)
 
     middle = lax.broadcasted_iota(jnp.int32, (1, DH), 1) < HALF - DH
 
@@ -271,9 +272,18 @@
 
         lax.fori_loop(0, each, step, 0)
 
-    def build_half(s, j):
-        prep_b(s, j)
-        loop(lambda p: build_kv(s, j, p), 4)
+    def build_all(*builds):
+        def body(p):
+            for build in builds:
+                build(p)
+
+        loop(body, 4 if len(builds) == 1 else 2)
+
+    def kv(s, j):
+        return lambda p: build_kv(s, j, p)
+
+    def q(j):
+        return lambda p: build_q(j, p)
 
     def put(which, p, state):
         m_acc[which, p], l_acc[which, p], o_acc[which, p] = state
@@ -282,7 +292,7 @@
         return m_acc[which, p], l_acc[which, p], o_acc[which, p]
 
     def scores_of(s, j_keys, j_queries, p):
-        return dot(kb[s, j_keys, p], qbd[j_queries, p])
+        return dot(kb[s][j_keys, p], qbd[j_queries, p])
 
     def own_blocks(p):
         shape = (HALF, 2 * HALF)
@@ -292,7 +302,7 @@
         low = jnp.where(seen, scores_of(0, jl0, jl0, p), MASKED)
         cross = scores_of(0, jl0, 1 - jl0, p)
         high = jnp.where(seen, scores_of(0, 1 - jl0, 1 - jl0, p), MASKED)
-        v_low, v_high = vb[0, jl0, p], vb[0, 1 - jl0, p]
+        v_low, v_high = vb[0][jl0, p], vb[0][1 - jl0, p]
         return [(low, v_low)], [(cross, v_low), (high, v_high)]
 
     def choose(s):
@@ -300,7 +310,7 @@
         pick = (lows > low0).astype(jnp.int32)
         return s, jls, jls + pick - 2 * jls * pick, jl0 + pick - 2 * jl0 * pick, pick == 1
 
-    def attend(offsets, width, last=False):
+    def attend(offsets, also, last=False):
         chosen = [choose(s) for s in offsets]
 
         def body(p):
@@ -314,9 +324,9 @@
                 low_tops, high_tops = [], []
             floating = []
             for s, jls, jk, jq, is_high in chosen:
-                high_blocks.append((scores_of(s, jls, 1 - jl0, p), vb[s, jls, p]))
+                high_blocks.append((scores_of(s, jls, 1 - jl0, p), vb[s][jls, p]))
                 scores = scores_of(s, jk, jq, p)
-                floating.append((scores, vb[s, jk, p], is_high))
+                floating.append((scores, vb[s][jk, p], is_high))
                 top = highest(scores)
                 high_tops.append(jnp.where(is_high, top, MASKED))
                 low_tops.append(jnp.where(is_high, MASKED, top))
@@ -327,6 +337,8 @@
                 low = jnp.maximum(low, top)
             for top in high_tops[1:]:
                 high = jnp.maximum(high, top)
+            for built in also:
+                build_kv(*built, p)
             low_parts = [weigh(scores, low, values) for scores, values in low_blocks]
             high_parts = [weigh(scores, high, values) for scores, values in high_blocks]
             for scores, values, is_high in floating:
@@ -361,7 +373,7 @@
 
             return store
 
-        loop(body, width)
+        loop(body, 2)
 
     def turned_rows(x):
         parts = [turn(x[:, i * DH : (i + 1) * DH]) for i in range(3)]
@@ -372,36 +384,38 @@
 
     jl0, low0 = scalars(0)
     prep_a(0)
+    prep_b(0, h)
     prep_aq()
-    build_half(0, h)
+    prep_q(h)
+    build_all(kv(0, h), q(h))
     pass_on(kv_out, kv_on)
-    prep_q(h)
-    loop(lambda p: build_q(h, p), 1)
+    wait_a(1)
+    prep_a(1)
+    prep_b(1, h)
     pass_on(q_out, q_on)
     wait_all(kv_on)
     send_b(0)
-    build_half(0, other)
-    wait_a(1)
+    prep_b(0, other)
+    build_all(kv(0, other), kv(1, h))
+    wait_a(2)
+    wait_b(1)
+    prep_b(1, other)
     wait_all(q_on)
     prep_q(other)
-    loop(lambda p: build_q(other, p), 1)
-    prep_a(1)
-    build_half(1, h)
-    attend([], 2)
-    wait_a(2)
-    wait_b(1)
-    build_half(1, other)
+    build_all(kv(1, other), q(other))
     prep_a(2)
-    build_half(2, h)
+    prep_b(2, h)
     wait_b(2)
-    attend([1], 4)
-    build_half(2, other)
+    prep_b(2, other)
+    attend([], [(2, h), (2, other)])
     wait_a(3)
     prep_a(3)
-    build_half(3, h)
+    prep_b(3, h)
+    attend([1], [(3, h)])
     wait_b(3)
-    build_half(3, other)
-    attend([2, 3], 2, last=True)
+    prep_b(3, other)
+    build_all(kv(3, other))
+    attend([2, 3], [], last=True)
     log0, log1 = logs[0], logs[1]
     log_ref[0:PAIRS] = jnp.where(first, log0, pltpu.roll(log1, HALF, 1))
     log_ref[PAIRS:] = jnp.where(first, pltpu.roll(log0, HALF, 1), log1)
@@ -451,8 +465,8 @@
             pltpu.VMEM((4, 2, 2 * DH, HALF), F32),
             pltpu.VMEM((4, 2, HALF, 4 * PAIRS), BF16),
             pltpu.VMEM((4, 2, 2, heads, HALF), F32),
-            pltpu.VMEM((4, 2, PAIRS, HALF, 2 * DH), BF16),
-            pltpu.VMEM((4, 2, PAIRS, 2 * DH, HALF), BF16),
+            *[pltpu.VMEM((2, PAIRS, HALF, 2 * DH), BF16)] * 4,
+            *[pltpu.VMEM((2, PAIRS, 2 * DH, HALF), BF16)] * 4,
             pltpu.VMEM((2, PAIRS, DH, rows), F32),
             pltpu.VMEM((2, PAIRS, 1, rows), F32),
             pltpu.VMEM((2, PAIRS, 1, rows), F32),

time: 53.5 us -> 53 us (level)
  the two profiles are of different devices: /device:TPU:24 before, /device:TPU:8 now
where the time goes in v7:
time: 53 us; the launch traced here: 52.8 us
  Pallas kernels  48.8 us (92%)
  local copies, waits for them, and re-layouts  3.32 us (6%)
  between operations  0.65 us (1%)
    pallas_call x1, Pallas kernels, on_device(): pl.pallas_call(kernel, out_shape=(jax.ShapeDtypeStruct((heads, rows, DH),...  48.8 us
    unnamed x4, local copies, waits for them, and re-layouts  3.32 us

profile of v7, /device:TPU:8, one launch (start us, length us, event | category | flops | bytes accessed | tf_op | source)
XLA Modules:
  0.0 52.8 jit_solution(3725741115950052743)
XLA Ops:
  0.6 48.8 %shard_map.86 = (bf16[16,384,128]{2,1,0:T(8,128)(2,1)}, f32[16,384]{1,0:T(8,128)}) custom-call(s32[1,2]{1,0:T(1,128)} %bt_in.1, bf16[6,16,384]{2,1,0:T(8,128)(2,1)} %aq_in.1, bf16[192,768]{1,0:T(8,128)(2,1)} %bq_in.1, bf16[2,16,384]{2,1,0:T(8,128)(2,1)} %ak_in.1, bf16[192,256]{1,0:T(8,128)(2,1)} %bk_in.1, bf16[2,16,384]{2,1,0:T(8,128)(2,1)} %av_in.1, ...), custom_call_target="tpu_custom_call" | custom-call | tf_op jit(solution)/shard_map/pallas_call | solution.py:442
  49.5 0.0 copy-start
  49.5 2.7 %copy.11 = bf16[16,384,128]{2,1,0:T(8,128)(2,1)} copy(bf16[16,384,128]{2,1,0:T(8,128)(2,1)} %get-tuple-element.4) | data formatting | bytes 3145728
  52.2 0.0 copy-done
  52.2 0.6 %copy.12 = f32[16,384]{1,0:T(8,128)} copy(f32[16,384]{1,0:T(8,128)S(1)} %copy-done) | data formatting | bytes 49152
Async XLA Ops:
  49.5 2.7 %copy-start = (f32[16,384]{1,0:T(8,128)S(1)}, f32[16,384]{1,0:T(8,128)}, u32[]{:S(2)}) copy-start(f32[16,384]{1,0:T(8,128)} %get-tuple-element.5) | copy-start | bytes 73732

commit v8 on v7

--- a/solution.py
+++ b/solution.py
@@ -383,35 +383,43 @@
         return pltpu.make_async_copy(out_ref.at[head], out_hbm.at[head], out_sem.at[head])
 
     jl0, low0 = scalars(0)
+    def on_core(which, wait, s):
+        @pl.when(core == which)
+        def _():
+            wait(s)
+
     prep_a(0)
     prep_b(0, h)
     prep_aq()
     prep_q(h)
     build_all(kv(0, h), q(h))
     pass_on(kv_out, kv_on)
-    wait_a(1)
-    prep_a(1)
-    prep_b(1, h)
+    on_core(1, wait_a, 1)
     pass_on(q_out, q_on)
     wait_all(kv_on)
     send_b(0)
     prep_b(0, other)
-    build_all(kv(0, other), kv(1, h))
-    wait_a(2)
+    wait_all(q_on)
+    prep_q(other)
+    build_all(kv(0, other), q(other))
+    on_core(0, wait_a, 1)
+    prep_a(1)
+    prep_b(1, h)
+    on_core(1, wait_a, 2)
     wait_b(1)
     prep_b(1, other)
-    wait_all(q_on)
-    prep_q(other)
-    build_all(kv(1, other), q(other))
+    build_all(kv(1, h), kv(1, other))
+    on_core(1, wait_b, 2)
+    on_core(0, wait_a, 2)
     prep_a(2)
     prep_b(2, h)
-    wait_b(2)
+    attend([], [(2, h)])
+    on_core(0, wait_b, 2)
     prep_b(2, other)
-    attend([], [(2, h), (2, other)])
     wait_a(3)
     prep_a(3)
     prep_b(3, h)
-    attend([1], [(3, h)])
+    attend([1], [(2, other), (3, h)])
     wait_b(3)
     prep_b(3, other)
     build_all(kv(3, other))

time: 53 us -> 54.9 us (1.036)
  the two profiles are of different devices: /device:TPU:8 before, /device:TPU:24 now
where the time goes in v8:
time: 54.9 us; the launch traced here: 54.3 us
  Pallas kernels  50.3 us (92%)
  local copies, waits for them, and re-layouts  3.32 us (6%)
  between operations  0.65 us (1%)
    pallas_call x1, Pallas kernels, on_device(): pl.pallas_call(kernel, out_shape=(jax.ShapeDtypeStruct((heads, rows, DH),...  50.3 us
    unnamed x4, local copies, waits for them, and re-layouts  3.32 us

profile of v8, /device:TPU:24, one launch (start us, length us, event | category | flops | bytes accessed | tf_op | source)
XLA Modules:
  0.0 54.3 jit_solution(3774632269340873592)
XLA Ops:
  0.6 50.3 %shard_map.86 = (bf16[16,384,128]{2,1,0:T(8,128)(2,1)}, f32[16,384]{1,0:T(8,128)}) custom-call(s32[1,2]{1,0:T(1,128)} %bt_in.1, bf16[6,16,384]{2,1,0:T(8,128)(2,1)} %aq_in.1, bf16[192,768]{1,0:T(8,128)(2,1)} %bq_in.1, bf16[2,16,384]{2,1,0:T(8,128)(2,1)} %ak_in.1, bf16[192,256]{1,0:T(8,128)(2,1)} %bk_in.1, bf16[2,16,384]{2,1,0:T(8,128)(2,1)} %av_in.1, ...), custom_call_target="tpu_custom_call" | custom-call | tf_op jit(solution)/shard_map/pallas_call | solution.py:450
  51.0 0.0 copy-start
  51.0 2.7 %copy.11 = bf16[16,384,128]{2,1,0:T(8,128)(2,1)} copy(bf16[16,384,128]{2,1,0:T(8,128)(2,1)} %get-tuple-element.4) | data formatting | bytes 3145728
  53.7 0.0 copy-done
  53.7 0.6 %copy.12 = f32[16,384]{1,0:T(8,128)} copy(f32[16,384]{1,0:T(8,128)S(1)} %copy-done) | data formatting | bytes 49152
Async XLA Ops:
  51.0 2.7 %copy-start = (f32[16,384]{1,0:T(8,128)S(1)}, f32[16,384]{1,0:T(8,128)}, u32[]{:S(2)}) copy-start(f32[16,384]{1,0:T(8,128)} %get-tuple-element.5) | copy-start | bytes 73732
